TPU v7x, 32 devices: a whole 2x2x4 slice. The times are simulated.
32 devices in a mesh: conv: 2 (over x), seq: 8 (over z, y), head: 2 (over core).
Axes of the slice: x: 2, y: 2, z: 4, core: 2. Of those that a mesh axis runs over, the one named last changes fastest.
Arguments:
- queries: bfloat16 [3072, 2048], P(('conv', 'seq'), 'head'), parts along dimension 0, may hold values from -10 to 10, as said below
- key_states: bfloat16 [3072, 512], P(('conv', 'seq'), 'head'), parts along dimension 0, may hold values from -5 to 5, as said below
- value_states: bfloat16 [3072, 512], P(('conv', 'seq'), 'head'), parts along dimension 0, may hold values from -16 to 16
- out_weight: bfloat16 [2048, 4096], P('head'), may hold values from -0.125 to 0.125
- turn_lengths: int32 [32], P('conv'), parts along dimension 0, may hold values from 1 to 959, as said below
- block_flags: int32 [16, 8], P(('conv', 'seq')), parts along dimension 0, may hold values 0 or 1
Outputs:
- pooled: float32 [32, 4096], P(('conv', 'seq'), 'head'), parts along dimension 0
There are 2 independent parts, one for each index of `conv`. A program takes and returns all parts, laid end to end along the dimension named above; an argument that names none is the same for every part. Nothing has to cross between parts.
Inputs may be any that keep to these rules, and one draw needn't show every extreme that they name: `queries`: every entry lies within the stated bounds. `key_states`: every entry lies within the stated bounds. `turn_lengths`: the lengths sum to 1536; turn 0 has one token and turn 1, the longest, has exactly 959 tokens.
All inputs are finite; a program needn't handle non-finite values. No bound on the sum of `block_flags` on one device may be relied on, other than what follows from the above.
Results may differ from a plain program's by a relative error of at most 0.0035.
Values may be sent and summed in bfloat16 or wider, within the bound.
No kernel may reach another device: no remote copies, remote signals or barrier semaphores. Data moves between devices by JAX's collectives and lax.ppermute only.
A program may use at most 128 MiB of HBM per device.

v0:
```python
import math

import jax
import jax.numpy as jnp
from jax import lax
from jax.sharding import PartitionSpec as P

HD = 128


big_negative = -1e30
log_two_e = 1.4426950408889634


def on_device(queries, key_states, value_states, out_weight, turn_lengths, block_flags):
    q_rows = queries.shape[0]
    heads_here = queries.shape[1] // HD
    groups = key_states.shape[1] // HD
    repeat = heads_here // groups
    factor = log_two_e / math.sqrt(HD)
    my_index = lax.axis_index("seq")
    own_pos = my_index * q_rows + jnp.arange(q_rows, dtype=jnp.int32)
    block_count = block_flags.shape[1]
    row_pick = jnp.zeros((q_rows,), jnp.int32)
    query_block = own_pos // q_rows
    grouped = queries.reshape(q_rows, groups, repeat, HD)

    def mask_for(key_start, length):
        key_pos = key_start + jnp.arange(length, dtype=jnp.int32)
        key_block = key_pos // q_rows
        hits = key_block[:, None] == jnp.arange(block_count, dtype=jnp.int32)[None, :]
        allowed = jnp.sum(jnp.where(hits[None], block_flags[:, None, :], 0), axis=2)
        allowed_rows = jnp.where(row_pick[:, None] == 1, allowed[-1][None, :], allowed[0][None, :])
        causal = key_pos[None, :] <= own_pos[:, None]
        return causal & ((key_block[None, :] == query_block[:, None]) | (allowed_rows == 1))

    def attend(state, key_rows, value_rows, key_start):
        run_top, run_sum, totals = state
        length = key_rows.shape[0]
        visible = mask_for(key_start, length)[None, None]
        logit = (
            jnp.einsum(
                "qgrd,kgd->grqk",
                grouped,
                key_rows.reshape(length, groups, HD),
                preferred_element_type=jnp.float32,
            )
            * factor
        )
        logit = jnp.where(visible, logit, big_negative)
        new_top = jnp.maximum(run_top, jnp.ceil(jnp.max(logit, axis=-1)))
        weights = jnp.where(visible, jnp.exp2(logit - new_top[..., None]), 0.0)
        rescale = jnp.exp2(run_top - new_top)
        run_sum = run_sum * rescale + jnp.sum(weights, axis=-1)
        update = jnp.einsum(
            "grqk,kgd->grqd",
            weights.astype(jnp.bfloat16),
            value_rows.reshape(length, groups, HD),
            preferred_element_type=jnp.float32,
        )
        totals = totals * rescale[..., None] + update
        return (new_top, run_sum, totals)

    start_state = (
        jnp.full((groups, repeat, q_rows), big_negative, jnp.float32),
        jnp.zeros((groups, repeat, q_rows), jnp.float32),
        jnp.zeros((groups, repeat, q_rows, HD), jnp.float32),
    )
    key_piece = lax.all_gather(key_states, "seq", axis=0, tiled=True)
    value_piece = lax.all_gather(value_states, "seq", axis=0, tiled=True)
    length = key_piece.shape[0]
    width_step = math.gcd(length, 1024)

    def one_block(number, carried):
        offset = number * width_step
        key_rows = lax.dynamic_slice_in_dim(key_piece, offset, width_step, 0)
        value_rows = lax.dynamic_slice_in_dim(value_piece, offset, width_step, 0)
        return attend(carried, key_rows, value_rows, offset)

    run_top, run_sum, totals = lax.fori_loop(0, length // width_step, one_block, start_state)
    attended_work = (
        (totals / run_sum[..., None])
        .transpose(2, 0, 1, 3)
        .reshape(q_rows, heads_here * HD)
        .astype(jnp.bfloat16)
    )
    turn_ends = jnp.cumsum(turn_lengths)
    starts = turn_ends - turn_lengths
    member = (starts[:, None] <= own_pos[None, :]) & (own_pos[None, :] < turn_ends[:, None])
    turn_share = jnp.where(member, 1.0, 0.0).astype(jnp.float32) / turn_lengths[:, None].astype(
        jnp.float32
    )
    partial_rows = jnp.dot(attended_work, out_weight, preferred_element_type=jnp.float32)
    projected_rows = lax.psum_scatter(partial_rows, "head", scatter_dimension=1, tiled=True)
    pooled_part = jnp.dot(turn_share, projected_rows, precision=lax.Precision.HIGHEST)
    return lax.psum_scatter(pooled_part, "seq", scatter_dimension=0, tiled=True)


def solution(mesh):
    in_specs = (
        P(("conv", "seq"), "head"),
        P(("conv", "seq"), "head"),
        P(("conv", "seq"), "head"),
        P("head", None),
        P("conv"),
        P(("conv", "seq"), None),
    )
    out_specs = P(("conv", "seq"), "head")
    return jax.shard_map(
        on_device, mesh=mesh, in_specs=in_specs, out_specs=out_specs, check_vma=False
    )
```

profile of v0, /device:TPU:0, one launch (start us, length us, event | category | flops | bytes accessed | tf_op | source)
XLA Modules:
  0.0 211.3 jit_solution(6904133844643909026)
XLA Ops:
  6.5 0.0 copy-start
  6.5 0.0 reduce-scatter.2.cloned.1.call-start
  6.5 36.3 %all_gather.6 = bf16[1536,256]{1,0:T(8,128)(2,1)} all-gather(bf16[192,256]{1,0:T(8,128)(2,1)} %param.9), channel_id=1, replica_groups=mesh['conv'=2,'seq'=8,'head'=2] {'seq'}, dimensions={0}, use_global_device_ids=true | all-gather | bytes 884736 | tf_op jit(solution)/shard_map/all_gather | solution.py:69
  42.9 34.2 %all_gather.7 = bf16[1536,256]{1,0:T(8,128)(2,1)} all-gather(bf16[192,256]{1,0:T(8,128)(2,1)} %param.10), channel_id=1, replica_groups=mesh['conv'=2,'seq'=8,'head'=2] {'seq'}, dimensions={0}, use_global_device_ids=true | all-gather | bytes 884736 | tf_op jit(solution)/shard_map/all_gather | solution.py:70
  77.1 1.3 reshape.229
  78.4 0.8 copy.26
  79.2 0.0 copy-done
  79.2 28.0 %while.22 = (s32[]{:T(128)}, f32[2,4,192]{2,1,0:T(4,128)S(1)}, f32[2,4,192]{2,1,0:T(4,128)S(1)}, f32[2,4,192,128]{3,2,1,0:T(8,128)}, s32[1,8]{1,0:T(1,128)S(1)},...) while((s32[]{:T(128)}, f32[2,4,192]{2,1,0:T(4,128)S(1)}, ...), condition=%wide.region_5.6_spmd.clone.clone.clone, body=%wide.region_1.5_spmd.clone.clone.clone.sunk | while | flops 415462080 | bytes 14534883 | solution.py:80
  79.2 0.1 select_reduce_fusion.2
  79.3 0.2 or_and_fusion.2
  79.5 1.1 constant_dynamic-slice_fusion.4
  80.6 0.8 copy.39
  81.4 1.8 fusion.54
  83.3 1.2 fusion.55
  84.5 0.8 copy.40
  85.3 3.1 %fusion.57 = f32[2,4,192,128]{3,2,1,0:T(8,128)} fusion(bf16[512,2,128,1]{0,2,3,1:T(8,128)(2,1)} %bitcast.53, f32[2,512,192,4]{1,2,3,0:T(8,128)S(1)} %get-tuple-element.465, f32[2,4,192]{2,1,0:T(4,128)S(1)} %ceil_maximum_fusion.2, pred[192,512]{1,0:T(8,128)(4,1)S(1)} %or_and_fusion.2, f32[2,4,192,128]{3,2,1,0:T(8,128)} %get-tuple-element.485, ...), kind=kOutput, calls=%fused_computation.9.clone.1 | convolution fusion | flops 206635008 | bytes 5091329 | tf_op jit(solution)/shard_map/while/body/eval_jaxpr/grqk,kgd->grqd/dot_general | solution.py:55
  88.5 0.1 select_reduce_fusion.2
  88.6 0.2 or_and_fusion.2
  88.8 1.1 constant_dynamic-slice_fusion.4
  89.8 0.8 copy.39
  90.7 1.8 fusion.54
  92.5 1.2 fusion.55
  93.8 0.8 copy.40
  94.6 3.2 %fusion.57 = f32[2,4,192,128]{3,2,1,0:T(8,128)} fusion(bf16[512,2,128,1]{0,2,3,1:T(8,128)(2,1)} %bitcast.53, f32[2,512,192,4]{1,2,3,0:T(8,128)S(1)} %get-tuple-element.465, f32[2,4,192]{2,1,0:T(4,128)S(1)} %ceil_maximum_fusion.2, pred[192,512]{1,0:T(8,128)(4,1)S(1)} %or_and_fusion.2, f32[2,4,192,128]{3,2,1,0:T(8,128)} %get-tuple-element.485, ...), kind=kOutput, calls=%fused_computation.9.clone.1 | convolution fusion | flops 206635008 | bytes 5091329 | tf_op jit(solution)/shard_map/while/body/eval_jaxpr/grqk,kgd->grqd/dot_general | solution.py:55
  97.8 0.1 select_reduce_fusion.2
  98.0 0.2 or_and_fusion.2
  98.1 1.1 constant_dynamic-slice_fusion.4
  99.2 0.8 copy.39
  100.1 1.8 fusion.54
  101.9 1.2 fusion.55
  103.1 0.8 copy.40
  104.0 3.2 %fusion.57 = f32[2,4,192,128]{3,2,1,0:T(8,128)} fusion(bf16[512,2,128,1]{0,2,3,1:T(8,128)(2,1)} %bitcast.53, f32[2,512,192,4]{1,2,3,0:T(8,128)S(1)} %get-tuple-element.465, f32[2,4,192]{2,1,0:T(4,128)S(1)} %ceil_maximum_fusion.2, pred[192,512]{1,0:T(8,128)(4,1)S(1)} %or_and_fusion.2, f32[2,4,192,128]{3,2,1,0:T(8,128)} %get-tuple-element.485, ...), kind=kOutput, calls=%fused_computation.9.clone.1 | convolution fusion | flops 206635008 | bytes 5091329 | tf_op jit(solution)/shard_map/while/body/eval_jaxpr/grqk,kgd->grqd/dot_general | solution.py:55
  107.2 1.4 fusion.19
  108.6 0.3 copy.28
  108.9 0.3 convert_element_type.26
  109.2 6.9 %fusion.35 = f32[192,4096]{1,0:T(8,128)} fusion(bf16[192,1024]{1,0:T(8,128)(2,1)S(1)} %convert_element_type.26, bf16[1024,4096]{1,0:T(8,128)(2,1)} %param.11), kind=kOutput, calls=%fused_computation.51 | convolution fusion | flops 1610612736 | bytes 11927552 | tf_op jit(solution)/shard_map/dot_general | solution.py:93
  116.1 0.0 reduce-scatter.2.cloned.1.call-update
  116.1 0.0 all-reduce.3.cloned.1.call-start
  116.1 0.6 copy-done.1
  116.7 0.1 copy.24
  116.8 0.1 reduce.6
  117.0 11.5 %reduce-scatter.2.cloned.1.call-done = f32[192,2048]{1,0:T(8,128)} async-done(((f32[192,4096]{1,0:T(8,128)}), f32[192,2048]{1,0:T(8,128)}) %reduce-scatter.2.cloned.1.call-update) | async-done | bytes 1572880 | tf_op jit(solution)/shard_map/reduce_scatter | solution.py:94
  128.5 2.9 %fusion.20 = f32[16,2048]{1,0:T(8,128)} fusion(f32[192,2048]{1,0:T(8,128)} %reduce-scatter.2.cloned.1.call-done, f32[16]{0:T(128)S(1)} %get-tuple-element.393, s32[192]{0:T(256)S(1)} %iota_add_fusion.2, s32[16]{0:T(128)S(1)} %reduce.6, s32[16]{0:T(128)S(1)} %get-tuple-element.392), kind=kOutput, calls=%fused_computation.34 | convolution fusion | flops 75512832 | bytes 1704896 | tf_op jit(solution)/shard_map/dot_general | solution.py:95
  131.4 0.0 all-reduce.3.cloned.1.call-update
  131.4 0.0 copy-done.2
  131.4 0.6 dynamic-slice
  132.6 70.4 %all-reduce.3.cloned.1.call-done = f32[16,2048]{1,0:T(8,128)} async-done(((f32[16,2048]{1,0:T(8,128)}), f32[16,2048]{1,0:T(8,128)}) %all-reduce.3.cloned.1.call-update) | async-done | bytes 131088
  203.0 1.5 constant_dynamic-slice_fusion.2
  (26 shorter events, 0.2 us)
Async XLA Ops:
  6.5 72.6 %copy-start = (s32[1,8]{1,0:T(1,128)S(1)}, s32[1,8]{1,0:T(1,128)}, u32[]{:S(2)}) copy-start(s32[1,8]{1,0:T(1,128)} %param.13) | copy-start | bytes 100
  6.5 121.9 %reduce-scatter.2.cloned.1.call-start = ((), (), s32[]{:S(2)}) async-start(), calls=%async_computation.1 | async-start | bytes 4718592 | tf_op jit(solution)/shard_map/reduce_scatter | solution.py:94
  116.1 0.7 copy-start.1
  116.1 15.3 %copy-start.2 = (u32[32]{0:T(128)S(1)}, u32[32]{0:T(128)}, u32[]{:S(2)}) copy-start(u32[32]{0:T(128)} %constant.141) | copy-start | bytes 388
  116.1 86.9 %all-reduce.3.cloned.1.call-start = ((), (), s32[]{:S(2)}) async-start(), calls=%async_computation.2 | async-start | bytes 262144
Sparse Core Ops, SparseCore 0:
  116.2 12.2 reduce-scatter.1
  132.2 70.7 all-reduce.2
where the time goes:
time: 212 us; the launch traced here: 211 us
  waiting for transfers between devices  81.9 us (39%)
  blocking collectives  70.6 us (33%)
  matrix products  24.8 us (12%)
  between operations  14.1 us (7%)
  local copies, waits for them, and re-layouts  13.6 us (6%)
  other arithmetic  6.13 us (3%)
    unnamed x3, waiting for transfers between devices  70.4 us
    all_gather x1, blocking collectives, on_device(): key_piece = lax.all_gather(key_states, 'seq', axis=0, tiled=True)  36.3 us
    all_gather x1, blocking collectives, on_device(): value_piece = lax.all_gather(value_states, 'seq', axis=0, tiled=True)  34.2 us
    reduce_scatter x1, waiting for transfers between devices, on_device(): lax.psum_scatter(partial_rows, 'head', scatter_dimension=1, tiled=True)  11.5 us
    dot_general x3, matrix products, attend(): jnp.einsum('grqk,kgd->grqd', weights.astype(jnp.bfloat16), value_rows.res...  9.53 us
    dot_general x1, matrix products, on_device(): jnp.dot(attended_work, out_weight, preferred_element_type=jnp.float32)  6.85 us
    dynamic_slice x6, local copies, waits for them, and re-layouts, one_block(): value_rows = lax.dynamic_slice_in_dim(value_piece, offset, width_step, 0)  5.76 us
    dot_general x3, matrix products, attend(): jnp.einsum('qgrd,kgd->grqk', grouped, key_rows.reshape(length, groups, HD...  5.5 us
  transfers between devices with their start and end apart: 2, of which 2 were waited for; matrix products, arithmetic and copies ran while one was open for 0% of the time, Pallas kernels for 0%

commit v1 on v0

v1 whole, which is shorter than its diff:
```python
import functools
import math

import jax
import jax.numpy as jnp
from jax import lax
from jax.experimental import pallas as pl
from jax.experimental.pallas import tpu as pltpu
from jax.sharding import PartitionSpec as P

HD = 128

big_negative = -1e30
log_two_e = 1.4426950408889634

big_limit = 40 * 1024 * 1024
small_cost = pl.CostEstimate(flops=1024, bytes_accessed=1024, transcendentals=0)

in_vmem = pl.BlockSpec(memory_space=pltpu.VMEM)
in_smem = pl.BlockSpec(memory_space=pltpu.SMEM)
anywhere = pl.BlockSpec(memory_space=pl.ANY)


def place(across):
    index = lax.axis_index("seq")
    return index // across, lax.rem(index, across)


def block_at(z, y, e, across):
    return z * across + lax.rem(y - e + across, across)


def call(kernel, out_shape, **settings):
    limit = settings.pop("limit", 16 * 1024 * 1024)
    return pl.pallas_call(
        kernel,
        out_shape=out_shape,
        out_specs=jax.tree.map(lambda _: in_vmem, out_shape),
        compiler_params=pltpu.CompilerParams(vmem_limit_bytes=limit),
        cost_estimate=small_cost,
        **settings,
    )


def pack_keys_kernel(across, key_ref, value_ref, *outs_and_sem):
    outs, done = outs_and_sem[:-1], outs_and_sem[-1]
    _, y = place(across)
    copies = []
    for e, out_ref in enumerate(outs):
        start = pl.multiple_of(lax.rem(y + e, across) * HD, HD)
        for i, ref in enumerate((key_ref, value_ref)):
            copies.append(
                pltpu.make_async_copy(
                    ref.at[:, pl.ds(start, HD)], out_ref.at[:, i * HD : (i + 1) * HD], done.at[2 * e + i]
                )
            )
    for copy in copies:
        copy.start()
    for copy in copies:
        copy.wait()


def pack_keys(across, keys, values):
    shape = jax.ShapeDtypeStruct((keys.shape[0], 2 * HD), keys.dtype)
    return call(
        functools.partial(pack_keys_kernel, across),
        [shape] * across,
        in_specs=[anywhere] * 2,
        scratch_shapes=[pltpu.SemaphoreType.DMA((2 * across,))],
    )(keys, values)


def pack_queries_kernel(across, flags_at, meta_ref, query_ref, after_ref, *outs_and_sem):
    del after_ref
    outs, done = outs_and_sem[:-1], outs_and_sem[-1]
    _, y = place(across)
    q_rows, width = query_ref.shape
    mine = width // across
    copies = []
    for e, out_ref in enumerate(outs):
        start = pl.multiple_of(lax.rem(y + e, across) * mine, mine)
        copies.append(
            pltpu.make_async_copy(
                query_ref.at[:, pl.ds(start, mine)], out_ref.at[0:q_rows, :], done.at[e]
            )
        )
    for copy in copies:
        copy.start()
    count = meta_ref.shape[0] - flags_at
    padded = outs[0].shape[0] - q_rows
    number = lax.broadcasted_iota(jnp.int32, (padded, mine), 0)
    flags = jnp.zeros((padded, mine), jnp.float32)
    for j in range(count):
        flags = jnp.where((number == j) & (meta_ref[flags_at + j] == 1), 1.0, flags)
    for out_ref in outs:
        out_ref[q_rows:, :] = flags.astype(out_ref.dtype)
    for copy in copies:
        copy.wait()


def pack_queries(across, flags_at, meta, queries, after):
    q_rows, width = queries.shape
    padded = -(-(meta.shape[0] - flags_at) // 16) * 16
    shape = jax.ShapeDtypeStruct((q_rows + padded, width // across), queries.dtype)
    return call(
        functools.partial(pack_queries_kernel, across, flags_at),
        [shape] * across,
        in_specs=[in_smem, anywhere, anywhere],
        scratch_shapes=[pltpu.SemaphoreType.DMA((across,))],
    )(meta, queries, after)


def join_kernel(*refs):
    *parts, out_ref = refs
    rows = parts[0].shape[0]
    for e, part in enumerate(parts):
        out_ref[e * rows : (e + 1) * rows, :] = part[...]


def join(parts):
    rows, width = parts[0].shape
    shape = jax.ShapeDtypeStruct((rows * len(parts), width), parts[0].dtype)
    return call(join_kernel, shape, in_specs=[in_vmem] * len(parts))(*parts)


def row_update(turned_ref, kv_ref, switches, state, first):
    top, total_sum, totals = state
    across, _, columns = turned_ref.shape
    rows = kv_ref.shape[0] // across
    factor = log_two_e / math.sqrt(HD)
    keys = kv_ref[:, :HD]
    values = kv_ref[:, HD:].T
    logits = [
        jnp.dot(keys, turned_ref[e], preferred_element_type=jnp.float32) for e in range(across)
    ]
    if first:
        key_pos = lax.broadcasted_iota(jnp.int32, (rows, 1), 0)
        column = lax.broadcasted_iota(jnp.int32, (1, columns), 1)
        causal = key_pos <= lax.rem(column, rows)
    for e in range(across):
        blocks = [logits[e][b * rows : (b + 1) * rows] for b in range(across)]
        if first:
            blocks[e] = jnp.where(causal, blocks[e], big_negative)
        new_top = None if first else top[e]
        for b in range(across):
            block_top = jnp.ceil(jnp.max(blocks[b], axis=0, keepdims=True) * factor)
            if switches[e][b] is not None:
                block_top = jnp.where(switches[e][b], block_top, big_negative)
            new_top = block_top if new_top is None else jnp.maximum(new_top, block_top)
        weights, block_sum = [], None
        for b in range(across):
            against = new_top
            if switches[e][b] is not None:
                against = jnp.where(switches[e][b], new_top, -big_negative)
            weights.append(jnp.exp2(blocks[b] * factor - against))
            part = jnp.sum(weights[b], axis=0, keepdims=True)
            block_sum = part if block_sum is None else block_sum + part
        weights = jnp.concatenate([w.astype(jnp.bfloat16) for w in weights], axis=0)
        update = jnp.dot(values, weights, preferred_element_type=jnp.float32)
        if not first:
            rescale = jnp.exp2(top[e] - new_top)
            block_sum = total_sum[e] * rescale + block_sum
            update = totals[e] * rescale + update
        top[e] = new_top
        total_sum[e] = block_sum
        totals[e] = update


def switch_of(flags_ref, e, owner, columns, allowed=None):
    padded = flags_ref.shape[0] // 2
    flag = flags_ref[pl.ds(e * padded + jnp.maximum(owner, 0), 1), :]
    if allowed is not None:
        flag = flag * jnp.where(allowed, 1.0, 0.0)
    return jnp.concatenate([flag] * (columns // HD), axis=1) > 0.5


def first_kernel(across, turns, meta_ref, *refs):
    queries, refs = refs[:across], refs[across:]
    kv_ref, weight_ref, turned_ref, flags_ref, member_ref, inverse_ref, weight_out = refs[:7]
    state, rows_ref, copied = refs[7:10], refs[10], refs[11]
    weight_copy = pltpu.make_async_copy(weight_ref, weight_out, copied)
    weight_copy.start()
    z, y = place(across)
    q_rows = kv_ref.shape[0] // across
    repeat = queries[0].shape[1] // HD
    columns = repeat * q_rows
    padded = queries[0].shape[0] - q_rows
    for e in range(across):
        for r in range(repeat):
            turned_ref[e, :, r * q_rows : (r + 1) * q_rows] = queries[e][
                0:q_rows, r * HD : (r + 1) * HD
            ].T
        flags_ref[e * padded : (e + 1) * padded, :] = queries[e][q_rows:, 0:HD].astype(jnp.float32)
    owners = [block_at(z, y, e, across) for e in range(across)]
    switches = [
        [
            None if e == b else switch_of(flags_ref, e, owners[b], columns, owners[b] < owners[e])
            for b in range(across)
        ]
        for e in range(across)
    ]
    row_update(turned_ref, kv_ref, switches, state, True)

    column = lax.broadcasted_iota(jnp.int32, (1, columns), 1)
    for e in range(across):
        position = lax.rem(column, q_rows) + owners[e] * q_rows
        start = jnp.int32(0)
        for t in range(turns):
            length = meta_ref[1 + t]
            inside = (position >= start) & (position < start + length)
            rows_ref[t : t + 1, :] = jnp.where(inside, 1.0, 0.0)
            if e == 0:
                count = jnp.full((1, HD), length, jnp.int32).astype(jnp.float32)
                inverse_ref[t : t + 1, :] = 1.0 / count
            start = start + length
        for r in range(repeat):
            mine = (column >= r * q_rows) & (column < (r + 1) * q_rows)
            member_ref[e, r * turns : (r + 1) * turns, :] = jnp.where(
                mine, rows_ref[...], 0.0
            ).astype(jnp.bfloat16)
    weight_copy.wait()


def attend_first(across, turns, meta, queries, rows, weight):
    q_rows = rows.shape[0] // across
    padded = queries[0].shape[0] - q_rows
    repeat = queries[0].shape[1] // HD
    columns = repeat * q_rows
    f32, b16 = jnp.float32, jnp.bfloat16
    return call(
        functools.partial(first_kernel, across, turns),
        [
            jax.ShapeDtypeStruct((across, HD, columns), b16),
            jax.ShapeDtypeStruct((across * padded, HD), f32),
            jax.ShapeDtypeStruct((across, repeat * turns, columns), b16),
            jax.ShapeDtypeStruct((turns, HD), f32),
            jax.ShapeDtypeStruct(weight.shape, weight.dtype),
            jax.ShapeDtypeStruct((across, 1, columns), f32),
            jax.ShapeDtypeStruct((across, 1, columns), f32),
            jax.ShapeDtypeStruct((across, HD, columns), f32),
        ],
        in_specs=[in_smem] + [in_vmem] * (across + 1) + [anywhere],
        scratch_shapes=[pltpu.VMEM((turns, columns), f32), pltpu.SemaphoreType.DMA(())],
        limit=big_limit,
    )(meta, *queries, rows, weight)


def next_kernel(across, distance, turns, last, turned_ref, flags_ref, kv_ref, *refs):
    state, refs = refs[:3], refs[3:]
    z, y = place(across)
    columns = turned_ref.shape[2]

    @pl.when(z >= distance)
    def _():
        owners = [block_at(z - distance, y, b, across) for b in range(across)]
        switches = [
            [switch_of(flags_ref, e, owners[b], columns) for b in range(across)]
            for e in range(across)
        ]
        row_update(turned_ref, kv_ref, switches, state, False)

    if last:
        member_ref, inverse_ref, out_ref = refs
        rows = out_ref.shape[1]
        pooled = None
        for e in range(across):
            attended = (state[2][e] / state[1][e]).astype(jnp.bfloat16)
            part = lax.dot_general(
                member_ref[e],
                attended,
                (((1,), (1,)), ((), ())),
                preferred_element_type=jnp.float32,
            )
            pooled = part if pooled is None else pooled + part
        for r in range(pooled.shape[0] // turns):
            mean = pooled[r * turns : (r + 1) * turns] * inverse_ref[...]
            for s in range(out_ref.shape[0]):
                out_ref[s, :, r * HD : (r + 1) * HD] = mean[s * rows : (s + 1) * rows]


def attend_next(across, distance, turns, turned, flags, rows, state, pool, out_piece):
    last = pool is not None
    args = [turned, flags, rows, *state]
    if last:
        args += list(pool)
        out_shape, aliases = [jax.ShapeDtypeStruct(out_piece, jnp.float32)], {}
    else:
        out_shape = [jax.ShapeDtypeStruct(part.shape, part.dtype) for part in state]
        aliases = {3 + i: i for i in range(len(state))}
    return call(
        functools.partial(next_kernel, across, distance, turns, last),
        out_shape,
        in_specs=[in_vmem] * len(args),
        input_output_aliases=aliases,
    )(*args)


def project_kernel(across, meta_ref, parts_ref, weight_ref, keep_ref, send_ref):
    my_head = meta_ref[0]
    groups = []
    for y in range(across):
        total = parts_ref[y]
        for s in range(y + across, parts_ref.shape[0], across):
            total = total + parts_ref[s]
        groups.append(total)
    total = jnp.concatenate(groups, axis=1)
    rows = total.shape[0]
    high = total.astype(jnp.bfloat16)
    low = (total - high.astype(jnp.float32)).astype(jnp.bfloat16)
    both = jnp.concatenate([high, low], axis=0)
    half = keep_ref.shape[1]
    step = math.gcd(half, 512)
    for out_ref, side in ((send_ref, 1 - my_head), (keep_ref, my_head)):
        for c in range(half // step):
            start = pl.multiple_of(side * half + c * step, step)
            product = jnp.dot(
                both, weight_ref[:, pl.ds(start, step)], preferred_element_type=jnp.float32
            )
            out_ref[:, c * step : (c + 1) * step] = product[:rows] + product[rows:]


def project(across, meta, parts, weight):
    shape = jax.ShapeDtypeStruct((parts.shape[1], weight.shape[1] // 2), jnp.float32)
    return call(
        functools.partial(project_kernel, across),
        [shape] * 2,
        in_specs=[in_smem, in_vmem, in_vmem],
    )(meta, parts, weight)


def on_device(count, queries, key_states, value_states, out_weight, turn_lengths, block_flags):
    across = key_states.shape[1] // HD
    down = count // across
    turns = turn_lengths.shape[0]

    def over(rows, shift):
        pairs = [(i, i - i % across + (i + shift) % across) for i in range(count)]
        return lax.ppermute(rows, "seq", pairs)

    def up(rows, distance):
        step = distance * across
        return lax.ppermute(rows, "seq", [(i, i + step) for i in range(count - step)])

    my_head = lax.axis_index("head").astype(jnp.int32)
    meta = jnp.concatenate([my_head[None], turn_lengths, block_flags[0]])
    mine, *others = pack_keys(across, key_states, value_states)
    rows = join([mine] + [over(other, shift + 1) for shift, other in enumerate(others)])
    below = [rows] + [up(rows, distance) for distance in range(1, down)]
    mine, *others = pack_queries(across, 1 + turns, meta, queries, mine)
    queries = [mine] + [over(other, shift + 1) for shift, other in enumerate(others)]
    turned, flags, member, inverse, weight, *state = attend_first(
        across, turns, meta, queries, rows, out_weight
    )
    out_piece = (count, turns // count, queries[0].shape[1])
    for distance in range(1, down):
        last = distance == down - 1
        state = attend_next(
            across,
            distance,
            turns,
            turned,
            flags,
            below[distance],
            state,
            (member, inverse) if last else None,
            out_piece,
        )
    parts = lax.all_to_all(state[0], "seq", split_axis=0, concat_axis=0, tiled=True)
    keep, send = project(across, meta, parts, weight)
    return keep + lax.ppermute(send, "head", [(0, 1), (1, 0)])


def solution(mesh):
    in_specs = (
        P(("conv", "seq"), "head"),
        P(("conv", "seq"), "head"),
        P(("conv", "seq"), "head"),
        P("head", None),
        P("conv"),
        P(("conv", "seq"), None),
    )
    out_specs = P(("conv", "seq"), "head")
    return jax.shard_map(
        functools.partial(on_device, mesh.shape["seq"]),
        mesh=mesh,
        in_specs=in_specs,
        out_specs=out_specs,
        check_vma=False,
    )
```

time: 212 us -> 47 us (0.22)
  waiting for transfers between devices: 81.9 us -> 2.92 us
  blocking collectives: 70.6 us -> 19.4 us
  matrix products: 24.8 us -> 0 us
  between operations: 14.1 us -> 0.1 us
  starting transfers between devices: 0.04 us -> 12.7 us
  local copies, waits for them, and re-layouts: 13.6 us -> 2.78 us
  Pallas kernels: 0 us -> 7.42 us
  other arithmetic: 6.13 us -> 1.36 us
    all_gather x2 -> x0, blocking collectives: 70.6 us -> none  [the longest x1 36.3 us: on_device(): key_piece = lax.all_gather(key_states, 'seq', axis=0, tiled=True)]
    unnamed x3 -> x0, waiting for transfers between devices: 70.4 us -> none
    dot_general x8 -> x0, matrix products: 24.8 us -> none  [the longest x3 9.53 us: attend(): jnp.einsum('grqk,kgd->grqd', weights.astype(jnp.bfloat16), value_rows.res...]
    all_to_all x0 -> x1, blocking collectives: none -> 19.4 us  [on_device(): lax.all_to_all(state[0], 'seq', split_axis=0, concat_axis=0, tiled=True)]
    ppermute x0 -> x6, starting transfers between devices: none -> 12.7 us  [the longest x3 9.59 us: up(): lax.ppermute(rows, 'seq', [(i, i + step) for i in range(count - step)])]
    reduce_scatter x1 -> x0, waiting for transfers between devices: 11.5 us -> none  [on_device(): lax.psum_scatter(partial_rows, 'head', scatter_dimension=1, tiled=True)]
    dynamic_slice x9 -> x0, local copies, waits for them, and re-layouts: 8.3 us -> none  [the longest x6 5.76 us: one_block(): value_rows = lax.dynamic_slice_in_dim(value_piece, offset, width_step, 0)]
    pallas_call x0 -> x8, Pallas kernels: none -> 7.42 us  [the longest x1 4.6 us: attend_first(): call(functools.partial(first_kernel, across, turns), [jax.ShapeDtypeStruc...]
  transfers between devices with their start and end apart: 2 -> 6, of which waited for: 2 -> 3; matrix products, arithmetic and copies ran while one was open for 0% -> 2% of each run, Pallas kernels for 0% -> 11%
where the time goes in v1:
time: 47 us; the launch traced here: 46.7 us
  blocking collectives  19.4 us (41%)
  starting transfers between devices  12.7 us (27%)
  Pallas kernels  7.42 us (16%)
  waiting for transfers between devices  2.92 us (6%)
  local copies, waits for them, and re-layouts  2.78 us (6%)
  other arithmetic  1.36 us (3%)
    all_to_all x1, blocking collectives, on_device(): lax.all_to_all(state[0], 'seq', split_axis=0, concat_axis=0, tiled=True)  19.4 us
    ppermute x3, starting transfers between devices, up(): lax.ppermute(rows, 'seq', [(i, i + step) for i in range(count - step)])  9.59 us
    pallas_call x1, Pallas kernels, attend_first(): call(functools.partial(first_kernel, across, turns), [jax.ShapeDtypeStruc...  4.6 us
    ppermute x2, starting transfers between devices, over(): return lax.ppermute(rows, 'seq', pairs)  3.12 us
    unnamed x6, local copies, waits for them, and re-layouts  2.78 us
    pallas_call x1, Pallas kernels, project(): call(functools.partial(project_kernel, across), [shape] * 2, in_specs=[in...  1.74 us
    ppermute x3, waiting for transfers between devices, up(): lax.ppermute(rows, 'seq', [(i, i + step) for i in range(count - step)])  1.42 us
    ppermute x1, waiting for transfers between devices, on_device(): return keep + lax.ppermute(send, 'head', [(0, 1), (1, 0)])  1.19 us
  transfers between devices with their start and end apart: 6, of which 3 were waited for; matrix products, arithmetic and copies ran while one was open for 2% of the time, Pallas kernels for 11%

profile of v1, /device:TPU:0, one launch (start us, length us, event | category | flops | bytes accessed | tf_op | source)
XLA Modules:
  0.0 46.7 jit_solution(14999375376117544100)
XLA Ops:
  0.0 0.0 copy-start.1
  0.0 0.9 %copy-done.1 = bf16[192,256]{1,0:T(8,128)(2,1)S(1)} copy-done((bf16[192,256]{1,0:T(8,128)(2,1)S(1)}, bf16[192,256]{1,0:T(8,128)(2,1)}, u32[]{:S(2)}) %copy-start.1) | copy-done | bytes 98328
  0.9 0.0 copy-start.2
  0.9 0.9 %copy-done.2 = bf16[192,256]{1,0:T(8,128)(2,1)S(1)} copy-done((bf16[192,256]{1,0:T(8,128)(2,1)S(1)}, bf16[192,256]{1,0:T(8,128)(2,1)}, u32[]{:S(2)}) %copy-start.2) | copy-done | bytes 98328
  1.8 0.1 shard_map.64
  1.9 3.0 %collective-permute-start.1 = (bf16[192,256]{1,0:T(8,128)(2,1)S(1)}, bf16[192,256]{1,0:T(8,128)(2,1)S(1)}, u32[]{:S(2)}, u32[]{:S(2)}) collective-permute-start(bf16[192,256]{1,0:T(8,128)(2,1)S(1)} %get-tuple-element.28), channel_id=1, source_target_pairs={{0,2},{2,0},{4,6},{6,4},{8,10},{10,8},{12,14},{14,12},{1,3},{3,1},... | collective-permute-start | bytes 294920 | tf_op jit(solution)/shard_map/ppermute | solution.py:338
  4.9 0.7 %pad_add_fusion.meta_ref = s32[25]{0:T(128)S(1)} fusion(s32[8]{0:T(128)} %bitcast.2, s32[16]{0:T(128)} %param.10, s32[1]{0:T(128)} %bitcast), kind=kLoop, calls=%fused_computation | loop fusion | flops 50 | bytes 200 | tf_op jit(solution)/shard_map/concatenate | solution.py:345
  5.7 0.0 copy-start
  5.7 1.0 %copy-done = bf16[192,1024]{1,0:T(8,128)(2,1)S(1)} copy-done((bf16[192,1024]{1,0:T(8,128)(2,1)S(1)}, bf16[192,1024]{1,0:T(8,128)(2,1)}, u32[]{:S(2)}) %copy-start) | copy-done | bytes 393240
  6.7 0.7 %shard_map.65 = (bf16[208,512]{1,0:T(8,128)(2,1)S(1)}, bf16[208,512]{1,0:T(8,128)(2,1)S(1)}) custom-call(s32[25]{0:T(128)S(1)} %pad_add_fusion.meta_ref, bf16[192,1024]{1,0:T(8,128)(2,1)S(1)} %copy-done, bf16[192,256]{1,0:T(8,128)(2,1)S(1)} %get-tuple-element.25.after_ref.refs_0_), custom_call_target="tpu_custom_call" | custom-call | flops 1024 | bytes 1024 | tf_op jit(solution)/shard_map/pallas_call | solution.py:105
  7.3 0.1 collective-permute-start
  7.4 0.3 collective-permute-done.1.refs_1_
  7.7 3.8 %collective-permute-start.4 = (bf16[384,256]{1,0:T(8,128)(2,1)S(1)}, bf16[384,256]{1,0:T(8,128)(2,1)S(1)}, u32[]{:S(2)}, u32[]{:S(2)}) collective-permute-start(bf16[384,256]{1,0:T(8,128)(2,1)S(1)} %shard_map.66.refs_2_), channel_id=1, source_target_pairs={{0,4},{2,6},{4,8},{6,10},{8,12},{10,14},{1,5},{3,7},{5,9},{7,11},{... | collective-permute-start | bytes 589832 | tf_op jit(solution)/shard_map/ppermute | solution.py:342
  11.5 4.5 %collective-permute-start.3 = (bf16[384,256]{1,0:T(8,128)(2,1)S(1)}, bf16[384,256]{1,0:T(8,128)(2,1)S(1)}, u32[]{:S(2)}, u32[]{:S(2)}) collective-permute-start(bf16[384,256]{1,0:T(8,128)(2,1)S(1)} %shard_map.66.refs_2_), channel_id=1, source_target_pairs={{0,8},{2,10},{4,12},{6,14},{1,9},{3,11},{5,13},{7,15},{16,24},{18,... | collective-permute-start | bytes 589832 | tf_op jit(solution)/shard_map/ppermute | solution.py:342
  16.0 1.3 %collective-permute-start.2 = (bf16[384,256]{1,0:T(8,128)(2,1)S(1)}, bf16[384,256]{1,0:T(8,128)(2,1)S(1)}, u32[]{:S(2)}, u32[]{:S(2)}) collective-permute-start(bf16[384,256]{1,0:T(8,128)(2,1)S(1)} %shard_map.66.refs_2_), channel_id=1, source_target_pairs={{0,12},{2,14},{1,13},{3,15},{16,28},{18,30},{17,29},{19,31}} | collective-permute-start | bytes 589832 | tf_op jit(solution)/shard_map/ppermute | solution.py:342
  17.3 0.0 collective-permute-done.refs_1_
  17.3 4.6 %shard_map.67 = (bf16[2,128,768]{2,1,0:T(8,128)(2,1)S(1)}, f32[32,128]{1,0:T(8,128)S(1)}, bf16[2,64,768]{2,1,0:T(8,128)(2,1)S(1)}, f32[16,128]{1,0:T(8,128)S(1)}...) custom-call(s32[25]{0:T(128)S(1)} %pad_add_fusion.meta_ref, ...), custom_call_target="tpu_custom_call" | custom-call | flops 1024 | bytes 1024 | tf_op jit(solution)/shard_map/pallas_call | solution.py:230
  22.0 0.0 collective-permute-done.4.kv_ref
  22.0 0.0 collective-permute-done.3.kv_ref
  22.0 1.4 %collective-permute-done.2.kv_ref = bf16[384,256]{1,0:T(8,128)(2,1)S(1)} collective-permute-done((bf16[384,256]{1,0:T(8,128)(2,1)S(1)}, bf16[384,256]{1,0:T(8,128)(2,1)S(1)}, u32[]{:S(2)}, u32[]{:S(2)}) %collective-permute-start.2) | collective-permute-done | bytes 196640 | tf_op jit(solution)/shard_map/ppermute | solution.py:342
  23.5 0.3 shard_map.70
  23.7 19.4 %all_to_all.5.parts_ref = f32[8,2,512]{2,1,0:T(2,128)S(1)} all-to-all(f32[8,2,512]{2,1,0:T(2,128)S(1)} %shard_map.70), channel_id=1, replica_groups=mesh['conv'=2,'seq'=8,'head'=2] {'seq'}, dimensions={0} | all-to-all | bytes 65536 | tf_op jit(solution)/shard_map/all_to_all | solution.py:368
  43.1 1.7 %shard_map.71 = (f32[2,2048]{1,0:T(2,128)S(1)}, f32[2,2048]{1,0:T(2,128)S(1)}) custom-call(s32[25]{0:T(128)S(1)} %pad_add_fusion.meta_ref, f32[8,2,512]{2,1,0:T(2,128)S(1)} %all_to_all.5.parts_ref, bf16[1024,4096]{1,0:T(8,128)(2,1)S(1)} %get-tuple-element.42.weight_ref), custom_call_target="tpu_custom_call" | custom-call | flops 1024 | bytes 1024 | tf_op jit(solution)/shard_map/pallas_call | solution.py:324
  44.8 0.0 collective-permute-start.5
  44.8 1.2 %collective-permute-done.5 = f32[2,2048]{1,0:T(2,128)S(1)} collective-permute-done((f32[2,2048]{1,0:T(2,128)S(1)}, f32[2,2048]{1,0:T(2,128)S(1)}, u32[]{:S(2)}, u32[]{:S(2)}) %collective-permute-start.5) | collective-permute-done | bytes 16416 | tf_op jit(solution)/shard_map/ppermute | solution.py:370
  46.0 0.6 %add.3 = f32[2,2048]{1,0:T(2,128)} add(f32[2,2048]{1,0:T(2,128)S(1)} %get-tuple-element.43, f32[2,2048]{1,0:T(2,128)S(1)} %collective-permute-done.5) | non-fusion elementwise | flops 4096 | bytes 49152 | tf_op jit(solution)/shard_map/add | solution.py:370
  (3 shorter events, 0.1 us)
Async XLA Ops:
  0.0 0.9 %copy-start.1 = (bf16[192,256]{1,0:T(8,128)(2,1)S(1)}, bf16[192,256]{1,0:T(8,128)(2,1)}, u32[]{:S(2)}) copy-start(bf16[192,256]{1,0:T(8,128)(2,1)} %key_ref.1) | copy-start | bytes 294916
  0.9 0.9 %copy-start.2 = (bf16[192,256]{1,0:T(8,128)(2,1)S(1)}, bf16[192,256]{1,0:T(8,128)(2,1)}, u32[]{:S(2)}) copy-start(bf16[192,256]{1,0:T(8,128)(2,1)} %value_ref.1) | copy-start | bytes 294916
  1.9 5.8 %collective-permute-start.1 = (bf16[192,256]{1,0:T(8,128)(2,1)S(1)}, bf16[192,256]{1,0:T(8,128)(2,1)S(1)}, u32[]{:S(2)}, u32[]{:S(2)}) collective-permute-start(bf16[192,256]{1,0:T(8,128)(2,1)S(1)} %get-tuple-element.28), channel_id=1, source_target_pairs={{0,2},{2,0},{4,6},{6,4},{8,10},{10,8},{12,14},{14,12},{1,3},{3,1},... | collective-permute-start | bytes 294920 | tf_op jit(solution)/shard_map/ppermute | solution.py:338
  5.7 1.0 %copy-start = (bf16[192,1024]{1,0:T(8,128)(2,1)S(1)}, bf16[192,1024]{1,0:T(8,128)(2,1)}, u32[]{:S(2)}) copy-start(bf16[192,1024]{1,0:T(8,128)(2,1)} %query_ref.1) | copy-start | bytes 1179652
  7.3 10.0 %collective-permute-start = (bf16[208,512]{1,0:T(8,128)(2,1)S(1)}, bf16[208,512]{1,0:T(8,128)(2,1)S(1)}, u32[]{:S(2)}, u32[]{:S(2)}) collective-permute-start(bf16[208,512]{1,0:T(8,128)(2,1)S(1)} %get-tuple-element.27), channel_id=1, source_target_pairs={{0,2},{2,0},{4,6},{6,4},{8,10},{10,8},{12,14},{14,12},{1,3},{3,1},... | collective-permute-start | bytes 638984 | tf_op jit(solution)/shard_map/ppermute | solution.py:338
  7.7 14.2 %collective-permute-start.4 = (bf16[384,256]{1,0:T(8,128)(2,1)S(1)}, bf16[384,256]{1,0:T(8,128)(2,1)S(1)}, u32[]{:S(2)}, u32[]{:S(2)}) collective-permute-start(bf16[384,256]{1,0:T(8,128)(2,1)S(1)} %shard_map.66.refs_2_), channel_id=1, source_target_pairs={{0,4},{2,6},{4,8},{6,10},{8,12},{10,14},{1,5},{3,7},{5,9},{7,11},{... | collective-permute-start | bytes 589832 | tf_op jit(solution)/shard_map/ppermute | solution.py:342
  11.5 10.5 %collective-permute-start.3 = (bf16[384,256]{1,0:T(8,128)(2,1)S(1)}, bf16[384,256]{1,0:T(8,128)(2,1)S(1)}, u32[]{:S(2)}, u32[]{:S(2)}) collective-permute-start(bf16[384,256]{1,0:T(8,128)(2,1)S(1)} %shard_map.66.refs_2_), channel_id=1, source_target_pairs={{0,8},{2,10},{4,12},{6,14},{1,9},{3,11},{5,13},{7,15},{16,24},{18,... | collective-permute-start | bytes 589832 | tf_op jit(solution)/shard_map/ppermute | solution.py:342
  16.0 7.4 %collective-permute-start.2 = (bf16[384,256]{1,0:T(8,128)(2,1)S(1)}, bf16[384,256]{1,0:T(8,128)(2,1)S(1)}, u32[]{:S(2)}, u32[]{:S(2)}) collective-permute-start(bf16[384,256]{1,0:T(8,128)(2,1)S(1)} %shard_map.66.refs_2_), channel_id=1, source_target_pairs={{0,12},{2,14},{1,13},{3,15},{16,28},{18,30},{17,29},{19,31}} | collective-permute-start | bytes 589832 | tf_op jit(solution)/shard_map/ppermute | solution.py:342
  44.8 1.2 %collective-permute-start.5 = (f32[2,2048]{1,0:T(2,128)S(1)}, f32[2,2048]{1,0:T(2,128)S(1)}, u32[]{:S(2)}, u32[]{:S(2)}) collective-permute-start(f32[2,2048]{1,0:T(2,128)S(1)} %get-tuple-element.44), channel_id=1, source_target_pairs={{0,1},{1,0},{2,3},{3,2},{4,5},{5,4},{6,7},{7,6},{8,9},{9,8},{10,11... | collective-permute-start | bytes 49160 | tf_op jit(solution)/shard_map/ppermute | solution.py:370

commit v2 on v1

v2 whole, which is shorter than its diff:
```python
import functools
import math

import jax
import jax.numpy as jnp
from jax import lax
from jax.experimental import pallas as pl
from jax.experimental.pallas import tpu as pltpu
from jax.sharding import PartitionSpec as P

HD = 128

big_negative = -1e30
log_two_e = 1.4426950408889634

big_limit = 40 * 1024 * 1024
small_cost = pl.CostEstimate(flops=1024, bytes_accessed=1024, transcendentals=0)

in_vmem = pl.BlockSpec(memory_space=pltpu.VMEM)
in_smem = pl.BlockSpec(memory_space=pltpu.SMEM)
anywhere = pl.BlockSpec(memory_space=pl.ANY)


def place(across):
    index = lax.axis_index("seq")
    return index // across, lax.rem(index, across)


def block_at(z, y, e, across):
    return z * across + lax.rem(y - e + across, across)


def call(kernel, out_shape, **settings):
    limit = settings.pop("limit", 16 * 1024 * 1024)
    return pl.pallas_call(
        kernel,
        out_shape=out_shape,
        out_specs=jax.tree.map(lambda _: in_vmem, out_shape),
        compiler_params=pltpu.CompilerParams(vmem_limit_bytes=limit),
        cost_estimate=small_cost,
        **settings,
    )


def pack_kernel(across, key_ref, value_ref, query_ref, flags_ref, *refs):
    heads, rows = refs[:across], refs[across : 2 * across]
    flags_read, flags_rows, done, read = refs[2 * across :]
    _, y = place(across)
    q_rows, width = query_ref.shape
    mine = width // across
    sources = []
    for e in range(across):
        at = lax.rem(y + e, across)
        head = pl.ds(pl.multiple_of(at * HD, HD), HD)
        for i, ref in enumerate((key_ref, value_ref)):
            sources.append((ref.at[:, head], heads[e].at[:, i * HD : (i + 1) * HD]))
            sources.append((ref.at[:, head], rows[e].at[0:q_rows, i * HD : (i + 1) * HD]))
        group = pl.ds(pl.multiple_of(at * mine, mine), mine)
        sources.append((query_ref.at[:, group], rows[e].at[0:q_rows, 2 * HD : 2 * HD + mine]))
    flags_copy = pltpu.make_async_copy(flags_ref, flags_read, read)
    flags_copy.start()
    copies = [
        pltpu.make_async_copy(source, target, done.at[i])
        for i, (source, target) in enumerate(sources)
    ]
    for copy in copies:
        copy.start()
    flags_copy.wait()
    number = lax.broadcasted_iota(jnp.int32, flags_rows.shape, 0)
    flags = jnp.zeros(number.shape, jnp.float32)
    for j in range(flags_read.shape[1]):
        flags = jnp.where((number == j) & (flags_read[0, j] == 1), 1.0, flags)
    flags_rows[...] = flags.astype(flags_rows.dtype)
    for e in range(across):
        copy = pltpu.make_async_copy(flags_rows, rows[e].at[q_rows:, :], done.at[len(sources) + e])
        copy.start()
        copies.append(copy)
    for copy in copies:
        copy.wait()


def pack(across, keys, values, queries, flags):
    q_rows, width = queries.shape
    padded = -(-flags.shape[1] // 16) * 16
    wide = 2 * HD + width // across
    head = jax.ShapeDtypeStruct((q_rows, 2 * HD), keys.dtype)
    row = jax.ShapeDtypeStruct((q_rows + padded, wide), keys.dtype)
    outs = pl.pallas_call(
        functools.partial(pack_kernel, across),
        out_shape=[head] * across + [row] * across,
        in_specs=[anywhere] * 4,
        out_specs=[anywhere] * (2 * across),
        scratch_shapes=[
            pltpu.SMEM(flags.shape, jnp.int32),
            pltpu.VMEM((padded, wide), keys.dtype),
            pltpu.SemaphoreType.DMA((6 * across,)),
            pltpu.SemaphoreType.DMA(()),
        ],
        cost_estimate=small_cost,
    )(keys, values, queries, flags)
    return outs[:across], outs[across:]


def row_update(turned_ref, blocks_of_row, switches, state, first):
    top, total_sum, totals = state
    across, _, columns = turned_ref.shape
    rows = blocks_of_row[0].shape[0]
    factor = log_two_e / math.sqrt(HD)
    keys = jnp.concatenate([kv_ref[0:rows, :HD] for kv_ref in blocks_of_row], axis=0)
    values = jnp.concatenate([kv_ref[0:rows, HD : 2 * HD] for kv_ref in blocks_of_row], axis=0).T
    logits = [
        jnp.dot(keys, turned_ref[e], preferred_element_type=jnp.float32) for e in range(across)
    ]
    if first:
        key_pos = lax.broadcasted_iota(jnp.int32, (rows, 1), 0)
        column = lax.broadcasted_iota(jnp.int32, (1, columns), 1)
        causal = key_pos <= lax.rem(column, rows)
    for e in range(across):
        blocks = [logits[e][b * rows : (b + 1) * rows] for b in range(across)]
        if first:
            blocks[e] = jnp.where(causal, blocks[e], big_negative)
        new_top = None if first else top[e]
        for b in range(across):
            block_top = jnp.ceil(jnp.max(blocks[b], axis=0, keepdims=True) * factor)
            if switches[e][b] is not None:
                block_top = jnp.where(switches[e][b], block_top, big_negative)
            new_top = block_top if new_top is None else jnp.maximum(new_top, block_top)
        weights, block_sum = [], None
        for b in range(across):
            against = new_top
            if switches[e][b] is not None:
                against = jnp.where(switches[e][b], new_top, -big_negative)
            weights.append(jnp.exp2(blocks[b] * factor - against))
            part = jnp.sum(weights[b], axis=0, keepdims=True)
            block_sum = part if block_sum is None else block_sum + part
        weights = jnp.concatenate([w.astype(jnp.bfloat16) for w in weights], axis=0)
        update = jnp.dot(values, weights, preferred_element_type=jnp.float32)
        if not first:
            rescale = jnp.exp2(top[e] - new_top)
            block_sum = total_sum[e] * rescale + block_sum
            update = totals[e] * rescale + update
        top[e] = new_top
        total_sum[e] = block_sum
        totals[e] = update


def switch_of(flags_ref, e, owner, columns, allowed=None):
    padded = flags_ref.shape[0] // 2
    flag = flags_ref[pl.ds(e * padded + jnp.maximum(owner, 0), 1), :]
    if allowed is not None:
        flag = flag * jnp.where(allowed, 1.0, 0.0)
    return jnp.concatenate([flag] * (columns // HD), axis=1) > 0.5


def first_kernel(across, turns, q_rows, after, meta_ref, *refs):
    row, refs = refs[:across], refs[across + after :]
    weight_ref, turned_ref, flags_ref, member_ref, inverse_ref, weight_out = refs[:6]
    state, rows_ref, copied = refs[6:9], refs[9], refs[10]
    pieces = copied.shape[0]
    depth = weight_ref.shape[0] // pieces
    weight_copies = [
        pltpu.make_async_copy(
            weight_ref.at[i * depth : (i + 1) * depth],
            weight_out.at[i * depth : (i + 1) * depth],
            copied.at[i],
        )
        for i in range(pieces)
    ]
    for copy in weight_copies:
        copy.start()
    z, y = place(across)
    repeat = row[0].shape[1] // HD - 2
    columns = repeat * q_rows
    padded = row[0].shape[0] - q_rows
    for e in range(across):
        for r in range(repeat):
            turned_ref[e, :, r * q_rows : (r + 1) * q_rows] = row[e][
                0:q_rows, (2 + r) * HD : (3 + r) * HD
            ].T
        flags_ref[e * padded : (e + 1) * padded, :] = row[e][q_rows:, 0:HD].astype(jnp.float32)
    owners = [block_at(z, y, e, across) for e in range(across)]
    switches = [
        [
            None if e == b else switch_of(flags_ref, e, owners[b], columns, owners[b] < owners[e])
            for b in range(across)
        ]
        for e in range(across)
    ]
    row_update(turned_ref, [ref.at[0:q_rows, 0 : 2 * HD] for ref in row], switches, state, True)

    column = lax.broadcasted_iota(jnp.int32, (1, columns), 1)
    for e in range(across):
        position = lax.rem(column, q_rows) + owners[e] * q_rows
        start = jnp.int32(0)
        for t in range(turns):
            length = meta_ref[1 + t]
            inside = (position >= start) & (position < start + length)
            rows_ref[t : t + 1, :] = jnp.where(inside, 1.0, 0.0)
            if e == 0:
                count = jnp.full((1, HD), length, jnp.int32).astype(jnp.float32)
                inverse_ref[t : t + 1, :] = 1.0 / count
            start = start + length
        for r in range(repeat):
            mine = (column >= r * q_rows) & (column < (r + 1) * q_rows)
            member_ref[e, r * turns : (r + 1) * turns, :] = jnp.where(
                mine, rows_ref[...], 0.0
            ).astype(jnp.bfloat16)
    for copy in weight_copies:
        copy.wait()


def attend_first(across, turns, q_rows, meta, row, weight, after):
    padded = row[0].shape[0] - q_rows
    repeat = row[0].shape[1] // HD - 2
    columns = repeat * q_rows
    f32, b16 = jnp.float32, jnp.bfloat16
    return call(
        functools.partial(first_kernel, across, turns, q_rows, len(after)),
        [
            jax.ShapeDtypeStruct((across, HD, columns), b16),
            jax.ShapeDtypeStruct((across * padded, HD), f32),
            jax.ShapeDtypeStruct((across, repeat * turns, columns), b16),
            jax.ShapeDtypeStruct((turns, HD), f32),
            jax.ShapeDtypeStruct(weight.shape, weight.dtype),
            jax.ShapeDtypeStruct((across, 1, columns), f32),
            jax.ShapeDtypeStruct((across, 1, columns), f32),
            jax.ShapeDtypeStruct((across, HD, columns), f32),
        ],
        in_specs=[in_smem] + [in_vmem] * across + [anywhere] * (len(after) + 1),
        scratch_shapes=[pltpu.VMEM((turns, columns), f32), pltpu.SemaphoreType.DMA((8,))],
        limit=big_limit,
    )(meta, *row, *after, weight)


def next_kernel(across, distance, turns, last, turned_ref, flags_ref, *refs):
    row, state, refs = refs[:across], refs[across : across + 3], refs[across + 3 :]
    z, y = place(across)
    columns = turned_ref.shape[2]

    @pl.when(z >= distance)
    def _():
        owners = [block_at(z - distance, y, b, across) for b in range(across)]
        switches = [
            [switch_of(flags_ref, e, owners[b], columns) for b in range(across)]
            for e in range(across)
        ]
        row_update(turned_ref, row, switches, state, False)

    if last:
        member_ref, inverse_ref, out_ref = refs
        rows = out_ref.shape[1]
        pooled = None
        for e in range(across):
            attended = (state[2][e] / state[1][e]).astype(jnp.bfloat16)
            part = lax.dot_general(
                member_ref[e],
                attended,
                (((1,), (1,)), ((), ())),
                preferred_element_type=jnp.float32,
            )
            pooled = part if pooled is None else pooled + part
        for r in range(pooled.shape[0] // turns):
            mean = pooled[r * turns : (r + 1) * turns] * inverse_ref[...]
            for s in range(out_ref.shape[0]):
                out_ref[s, :, r * HD : (r + 1) * HD] = mean[s * rows : (s + 1) * rows]


def attend_next(across, distance, turns, turned, flags, row, state, pool, out_piece):
    last = pool is not None
    args = [turned, flags, *row, *state]
    if last:
        args += list(pool)
        out_shape, aliases = [jax.ShapeDtypeStruct(out_piece, jnp.float32)], {}
    else:
        out_shape = [jax.ShapeDtypeStruct(part.shape, part.dtype) for part in state]
        aliases = {2 + across + i: i for i in range(len(state))}
    return call(
        functools.partial(next_kernel, across, distance, turns, last),
        out_shape,
        in_specs=[in_vmem] * len(args),
        input_output_aliases=aliases,
    )(*args)


def project_kernel(across, other, meta_ref, parts_ref, weight_ref, out_ref):
    side = 1 - meta_ref[0] if other else meta_ref[0]
    groups = []
    for y in range(across):
        total = parts_ref[y]
        for s in range(y + across, parts_ref.shape[0], across):
            total = total + parts_ref[s]
        groups.append(total)
    total = jnp.concatenate(groups, axis=1)
    rows = total.shape[0]
    high = total.astype(jnp.bfloat16)
    low = (total - high.astype(jnp.float32)).astype(jnp.bfloat16)
    both = jnp.concatenate([high, low], axis=0)
    half = out_ref.shape[1]
    step = math.gcd(half, 512)
    for c in range(half // step):
        start = pl.multiple_of(side * half + c * step, step)
        product = jnp.dot(
            both, weight_ref[:, pl.ds(start, step)], preferred_element_type=jnp.float32
        )
        out_ref[:, c * step : (c + 1) * step] = product[:rows] + product[rows:]


def project(across, other, meta, parts, weight):
    return call(
        functools.partial(project_kernel, across, other),
        jax.ShapeDtypeStruct((parts.shape[1], weight.shape[1] // 2), jnp.float32),
        in_specs=[in_smem, in_vmem, in_vmem],
    )(meta, parts, weight)


def on_device(count, queries, key_states, value_states, out_weight, turn_lengths, block_flags):
    across = key_states.shape[1] // HD
    down = count // across
    turns = turn_lengths.shape[0]

    def send(rows, distance, shift):
        pairs = []
        for i in range(count - distance * across):
            z, y = i // across + distance, (i + shift) % across
            pairs.append((i, z * across + y))
        return lax.ppermute(rows, "seq", pairs)

    my_head = lax.axis_index("head").astype(jnp.int32)
    meta = jnp.concatenate([my_head[None], turn_lengths])
    parts, row = pack(across, key_states, value_states, queries, block_flags)
    below = [
        [send(parts[shift], distance, shift) for shift in range(across)]
        for distance in range(1, down)
    ]
    row = [row[0]] + [send(row[shift], 0, shift) for shift in range(1, across)]
    turned, flags, member, inverse, weight, *state = attend_first(
        across, turns, queries.shape[0], meta, row, out_weight, below[-1]
    )
    out_piece = (count, turns // count, queries.shape[1] // across)
    for distance in range(down - 1, 0, -1):
        last = distance == 1
        state = attend_next(
            across,
            distance,
            turns,
            turned,
            flags,
            below[distance - 1],
            state,
            (member, inverse) if last else None,
            out_piece,
        )
    parts = lax.all_to_all(state[0], "seq", split_axis=0, concat_axis=0, tiled=True)
    others = project(across, True, meta, parts, weight)
    others = lax.ppermute(others, "head", [(0, 1), (1, 0)])
    return project(across, False, meta, parts, weight) + others


def solution(mesh):
    in_specs = (
        P(("conv", "seq"), "head"),
        P(("conv", "seq"), "head"),
        P(("conv", "seq"), "head"),
        P("head", None),
        P("conv"),
        P(("conv", "seq"), None),
    )
    out_specs = P(("conv", "seq"), "head")
    return jax.shard_map(
        functools.partial(on_device, mesh.shape["seq"]),
        mesh=mesh,
        in_specs=in_specs,
        out_specs=out_specs,
        check_vma=False,
    )
```

time: 47 us -> 67.4 us (1.43)
  Pallas kernels: 7.42 us -> 32.6 us
  blocking collectives: 19.4 us -> 14.2 us
  starting transfers between devices: 12.7 us -> 17.7 us
  waiting for transfers between devices: 2.92 us -> 0.02 us
  local copies, waits for them, and re-layouts: 2.78 us -> 0.97 us
    pallas_call x5 -> x4, Pallas kernels: 7.09 us -> 32.3 us  [the longest x1 25 us: pack(): pl.pallas_call(functools.partial(pack_kernel, across), out_shape=[head] *...]
    all_to_all x1, blocking collectives: 19.4 us -> 14.2 us  [on_device(): lax.all_to_all(state[0], 'seq', split_axis=0, concat_axis=0, tiled=True)]
    ppermute x6 -> x8, starting transfers between devices: 12.7 us -> 17.7 us  [the longest x7 17.7 us: send(): return lax.ppermute(rows, 'seq', pairs)]
    ppermute x6 -> x8, waiting for transfers between devices: 2.92 us -> 0.02 us  [the longest x7 0.02 us: send(): return lax.ppermute(rows, 'seq', pairs)]
    unnamed x6 -> x2, local copies, waits for them, and re-layouts: 2.78 us -> 0.97 us
  transfers between devices with their start and end apart: 6 -> 8, of which waited for: 3 -> 0; matrix products, arithmetic and copies ran while one was open for 2% -> 1% of each run, Pallas kernels for 11% -> 9%
where the time goes in v2:
time: 67.4 us; the launch traced here: 67 us
  Pallas kernels  32.6 us (48%)
  starting transfers between devices  17.7 us (26%)
  blocking collectives  14.2 us (21%)
  other arithmetic  1.36 us (2%)
  local copies, waits for them, and re-layouts  0.97 us (1%)
    pallas_call x1, Pallas kernels, pack(): pl.pallas_call(functools.partial(pack_kernel, across), out_shape=[head] *...  25 us
    ppermute x7, starting transfers between devices, send(): return lax.ppermute(rows, 'seq', pairs)  17.7 us
    all_to_all x1, blocking collectives, on_device(): lax.all_to_all(state[0], 'seq', split_axis=0, concat_axis=0, tiled=True)  14.2 us
    pallas_call x1, Pallas kernels, attend_first(): call(functools.partial(first_kernel, across, turns, q_rows, len(after)),...  4.8 us
    pallas_call x2, Pallas kernels, project(): call(functools.partial(project_kernel, across, other), jax.ShapeDtypeStru...  2.41 us
  transfers between devices with their start and end apart: 8, of which 0 were waited for; matrix products, arithmetic and copies ran while one was open for 1% of the time, Pallas kernels for 9%

profile of v2, /device:TPU:0, one launch (start us, length us, event | category | flops | bytes accessed | tf_op | source)
XLA Modules:
  0.0 67.0 jit_solution(12942175108115072023)
XLA Ops:
  0.0 25.0 %shard_map.64 = (bf16[192,256]{1,0:T(8,128)(2,1)}, bf16[192,256]{1,0:T(8,128)(2,1)}, bf16[208,768]{1,0:T(8,128)(2,1)}, bf16[208,768]{1,0:T(8,128)(2,1)}) custom-call(bf16[192,256]{1,0:T(8,128)(2,1)} %key_ref.1, bf16[192,256]{1,0:T(8,128)(2,1)} %value_ref.1, bf16[192,1024]{1,0:T(8,128)(2,1)} %query_ref.1, s32[1,8]{1,0:T(1,128)} %flags_ref.1), custom_call_target="tpu_custom_call" | custom-call | flops 1024 | bytes 1024 | tf_op jit(solution)/shard_map/pallas_call | solution.py:88
  25.1 3.0 %collective-permute-start = (bf16[208,768]{1,0:T(8,128)(2,1)}, bf16[208,768]{1,0:T(8,128)(2,1)S(1)}, u32[]{:S(2)}, u32[]{:S(2)}) collective-permute-start(bf16[208,768]{1,0:T(8,128)(2,1)} %get-tuple-element.24), channel_id=1, source_target_pairs={{0,2},{2,0},{4,6},{6,4},{8,10},{10,8},{12,14},{14,12},{1,3},{3,1},... | collective-permute-start | bytes 958472 | tf_op jit(solution)/shard_map/ppermute | solution.py:326
  28.1 5.5 %collective-permute-start.1 = (bf16[192,256]{1,0:T(8,128)(2,1)}, bf16[192,256]{1,0:T(8,128)(2,1)S(1)}, u32[]{:S(2)}, u32[]{:S(2)}) collective-permute-start(bf16[192,256]{1,0:T(8,128)(2,1)} %get-tuple-element.25), channel_id=1, source_target_pairs={{0,12},{2,14},{1,13},{3,15},{16,28},{18,30},{17,29},{19,31}} | collective-permute-start | bytes 294920 | tf_op jit(solution)/shard_map/ppermute | solution.py:326
  33.6 1.3 %collective-permute-start.2 = (bf16[192,256]{1,0:T(8,128)(2,1)}, bf16[192,256]{1,0:T(8,128)(2,1)S(1)}, u32[]{:S(2)}, u32[]{:S(2)}) collective-permute-start(bf16[192,256]{1,0:T(8,128)(2,1)} %get-tuple-element.26), channel_id=1, source_target_pairs={{0,14},{2,12},{1,15},{3,13},{16,30},{18,28},{17,31},{19,29}} | collective-permute-start | bytes 294920 | tf_op jit(solution)/shard_map/ppermute | solution.py:326
  34.9 1.3 %collective-permute-start.5 = (bf16[192,256]{1,0:T(8,128)(2,1)}, bf16[192,256]{1,0:T(8,128)(2,1)S(1)}, u32[]{:S(2)}, u32[]{:S(2)}) collective-permute-start(bf16[192,256]{1,0:T(8,128)(2,1)} %get-tuple-element.25), channel_id=1, source_target_pairs={{0,8},{2,10},{4,12},{6,14},{1,9},{3,11},{5,13},{7,15},{16,24},{18,... | collective-permute-start | bytes 294920 | tf_op jit(solution)/shard_map/ppermute | solution.py:326
  36.2 1.3 %collective-permute-start.6 = (bf16[192,256]{1,0:T(8,128)(2,1)}, bf16[192,256]{1,0:T(8,128)(2,1)S(1)}, u32[]{:S(2)}, u32[]{:S(2)}) collective-permute-start(bf16[192,256]{1,0:T(8,128)(2,1)} %get-tuple-element.26), channel_id=1, source_target_pairs={{0,10},{2,8},{4,14},{6,12},{1,11},{3,9},{5,15},{7,13},{16,26},{18,... | collective-permute-start | bytes 294920 | tf_op jit(solution)/shard_map/ppermute | solution.py:326
  37.5 0.0 collective-permute-done.1.refs_2_.refs_0_
  37.5 2.5 %collective-permute-start.3 = (bf16[192,256]{1,0:T(8,128)(2,1)}, bf16[192,256]{1,0:T(8,128)(2,1)S(1)}, u32[]{:S(2)}, u32[]{:S(2)}) collective-permute-start(bf16[192,256]{1,0:T(8,128)(2,1)} %get-tuple-element.25), channel_id=1, source_target_pairs={{0,4},{2,6},{4,8},{6,10},{8,12},{10,14},{1,5},{3,7},{5,9},{7,11},{... | collective-permute-start | bytes 294920 | tf_op jit(solution)/shard_map/ppermute | solution.py:326
  40.0 0.0 collective-permute-done.2.refs_3_.refs_1_
  40.0 2.8 %collective-permute-start.4 = (bf16[192,256]{1,0:T(8,128)(2,1)}, bf16[192,256]{1,0:T(8,128)(2,1)S(1)}, u32[]{:S(2)}, u32[]{:S(2)}) collective-permute-start(bf16[192,256]{1,0:T(8,128)(2,1)} %get-tuple-element.26), channel_id=1, source_target_pairs={{0,6},{2,4},{4,10},{6,8},{8,14},{10,12},{1,7},{3,5},{5,11},{7,9},{... | collective-permute-start | bytes 294920 | tf_op jit(solution)/shard_map/ppermute | solution.py:326
  42.8 0.7 %pad_add_fusion.meta_ref = s32[17]{0:T(128)S(1)} fusion(s32[16]{0:T(128)} %param.10, s32[1]{0:T(128)} %bitcast), kind=kLoop, calls=%fused_computation | loop fusion | flops 17 | bytes 136 | tf_op jit(solution)/shard_map/concatenate | solution.py:329
  43.6 0.0 collective-permute-done.refs_1_
  43.6 0.0 copy-start
  43.6 1.0 %copy-done = bf16[208,768]{1,0:T(8,128)(2,1)S(1)} copy-done((bf16[208,768]{1,0:T(8,128)(2,1)S(1)}, bf16[208,768]{1,0:T(8,128)(2,1)}, u32[]{:S(2)}) %copy-start) | copy-done | bytes 319512
  44.5 4.8 %shard_map.65 = (bf16[2,128,768]{2,1,0:T(8,128)(2,1)S(1)}, f32[32,128]{1,0:T(8,128)S(1)}, bf16[2,64,768]{2,1,0:T(8,128)(2,1)S(1)}, f32[16,128]{1,0:T(8,128)S(1)}...) custom-call(s32[17]{0:T(128)S(1)} %pad_add_fusion.meta_ref, ...), custom_call_target="tpu_custom_call" | custom-call | flops 1024 | bytes 1024 | tf_op jit(solution)/shard_map/pallas_call | solution.py:217
  49.4 0.0 collective-permute-done.5.refs_0_
  49.4 0.0 collective-permute-done.6.refs_1_
  49.4 0.0 collective-permute-done.3.refs_0_
  49.4 0.0 collective-permute-done.4.refs_1_
  49.4 0.3 shard_map.68
  49.7 14.2 %all_to_all.5.parts_ref = f32[8,2,512]{2,1,0:T(2,128)S(1)} all-to-all(f32[8,2,512]{2,1,0:T(2,128)S(1)} %shard_map.68), channel_id=1, replica_groups=mesh['conv'=2,'seq'=8,'head'=2] {'seq'}, dimensions={0} | all-to-all | bytes 65536 | tf_op jit(solution)/shard_map/all_to_all | solution.py:353
  63.9 1.2 %shard_map.70 = f32[2,2048]{1,0:T(2,128)S(1)} custom-call(s32[17]{0:T(128)S(1)} %pad_add_fusion.meta_ref, f32[8,2,512]{2,1,0:T(2,128)S(1)} %all_to_all.5.parts_ref, bf16[1024,4096]{1,0:T(8,128)(2,1)S(1)} %get-tuple-element.40.weight_ref), custom_call_target="tpu_custom_call" | custom-call | flops 1024 | bytes 1024 | tf_op jit(solution)/shard_map/pallas_call | solution.py:309
  65.1 0.0 collective-permute-start.7
  65.1 1.2 %shard_map.69 = f32[2,2048]{1,0:T(2,128)S(1)} custom-call(s32[17]{0:T(128)S(1)} %pad_add_fusion.meta_ref, f32[8,2,512]{2,1,0:T(2,128)S(1)} %all_to_all.5.parts_ref, bf16[1024,4096]{1,0:T(8,128)(2,1)S(1)} %get-tuple-element.40.weight_ref), custom_call_target="tpu_custom_call" | custom-call | flops 1024 | bytes 1024 | tf_op jit(solution)/shard_map/pallas_call | solution.py:309
  66.3 0.0 collective-permute-done.7
  66.3 0.6 add.3
  (2 shorter events, 0.0 us)
Async XLA Ops:
  25.1 18.5 %collective-permute-start = (bf16[208,768]{1,0:T(8,128)(2,1)}, bf16[208,768]{1,0:T(8,128)(2,1)S(1)}, u32[]{:S(2)}, u32[]{:S(2)}) collective-permute-start(bf16[208,768]{1,0:T(8,128)(2,1)} %get-tuple-element.24), channel_id=1, source_target_pairs={{0,2},{2,0},{4,6},{6,4},{8,10},{10,8},{12,14},{14,12},{1,3},{3,1},... | collective-permute-start | bytes 958472 | tf_op jit(solution)/shard_map/ppermute | solution.py:326
  28.1 9.4 %collective-permute-start.1 = (bf16[192,256]{1,0:T(8,128)(2,1)}, bf16[192,256]{1,0:T(8,128)(2,1)S(1)}, u32[]{:S(2)}, u32[]{:S(2)}) collective-permute-start(bf16[192,256]{1,0:T(8,128)(2,1)} %get-tuple-element.25), channel_id=1, source_target_pairs={{0,12},{2,14},{1,13},{3,15},{16,28},{18,30},{17,29},{19,31}} | collective-permute-start | bytes 294920 | tf_op jit(solution)/shard_map/ppermute | solution.py:326
  33.6 6.4 %collective-permute-start.2 = (bf16[192,256]{1,0:T(8,128)(2,1)}, bf16[192,256]{1,0:T(8,128)(2,1)S(1)}, u32[]{:S(2)}, u32[]{:S(2)}) collective-permute-start(bf16[192,256]{1,0:T(8,128)(2,1)} %get-tuple-element.26), channel_id=1, source_target_pairs={{0,14},{2,12},{1,15},{3,13},{16,30},{18,28},{17,31},{19,29}} | collective-permute-start | bytes 294920 | tf_op jit(solution)/shard_map/ppermute | solution.py:326
  34.9 14.5 %collective-permute-start.5 = (bf16[192,256]{1,0:T(8,128)(2,1)}, bf16[192,256]{1,0:T(8,128)(2,1)S(1)}, u32[]{:S(2)}, u32[]{:S(2)}) collective-permute-start(bf16[192,256]{1,0:T(8,128)(2,1)} %get-tuple-element.25), channel_id=1, source_target_pairs={{0,8},{2,10},{4,12},{6,14},{1,9},{3,11},{5,13},{7,15},{16,24},{18,... | collective-permute-start | bytes 294920 | tf_op jit(solution)/shard_map/ppermute | solution.py:326
  36.2 13.2 %collective-permute-start.6 = (bf16[192,256]{1,0:T(8,128)(2,1)}, bf16[192,256]{1,0:T(8,128)(2,1)S(1)}, u32[]{:S(2)}, u32[]{:S(2)}) collective-permute-start(bf16[192,256]{1,0:T(8,128)(2,1)} %get-tuple-element.26), channel_id=1, source_target_pairs={{0,10},{2,8},{4,14},{6,12},{1,11},{3,9},{5,15},{7,13},{16,26},{18,... | collective-permute-start | bytes 294920 | tf_op jit(solution)/shard_map/ppermute | solution.py:326
  37.5 11.9 %collective-permute-start.3 = (bf16[192,256]{1,0:T(8,128)(2,1)}, bf16[192,256]{1,0:T(8,128)(2,1)S(1)}, u32[]{:S(2)}, u32[]{:S(2)}) collective-permute-start(bf16[192,256]{1,0:T(8,128)(2,1)} %get-tuple-element.25), channel_id=1, source_target_pairs={{0,4},{2,6},{4,8},{6,10},{8,12},{10,14},{1,5},{3,7},{5,9},{7,11},{... | collective-permute-start | bytes 294920 | tf_op jit(solution)/shard_map/ppermute | solution.py:326
  40.0 9.4 %collective-permute-start.4 = (bf16[192,256]{1,0:T(8,128)(2,1)}, bf16[192,256]{1,0:T(8,128)(2,1)S(1)}, u32[]{:S(2)}, u32[]{:S(2)}) collective-permute-start(bf16[192,256]{1,0:T(8,128)(2,1)} %get-tuple-element.26), channel_id=1, source_target_pairs={{0,6},{2,4},{4,10},{6,8},{8,14},{10,12},{1,7},{3,5},{5,11},{7,9},{... | collective-permute-start | bytes 294920 | tf_op jit(solution)/shard_map/ppermute | solution.py:326
  43.6 1.0 %copy-start = (bf16[208,768]{1,0:T(8,128)(2,1)S(1)}, bf16[208,768]{1,0:T(8,128)(2,1)}, u32[]{:S(2)}) copy-start(bf16[208,768]{1,0:T(8,128)(2,1)} %get-tuple-element.23.refs_0_) | copy-start | bytes 958468
  65.1 1.2 %collective-permute-start.7 = (f32[2,2048]{1,0:T(2,128)S(1)}, f32[2,2048]{1,0:T(2,128)S(1)}, u32[]{:S(2)}, u32[]{:S(2)}) collective-permute-start(f32[2,2048]{1,0:T(2,128)S(1)} %shard_map.70), channel_id=1, source_target_pairs={{0,1},{1,0},{2,3},{3,2},{4,5},{5,4},{6,7},{7,6},{8,9},{9,8},{10,11... | collective-permute-start | bytes 49160 | tf_op jit(solution)/shard_map/ppermute | solution.py:355

commit v3 on v2

--- a/solution.py
+++ b/solution.py
@@ -42,72 +42,37 @@
     )
 
 
-def pack_kernel(across, key_ref, value_ref, query_ref, flags_ref, *refs):
-    heads, rows = refs[:across], refs[across : 2 * across]
-    flags_read, flags_rows, done, read = refs[2 * across :]
-    _, y = place(across)
-    q_rows, width = query_ref.shape
-    mine = width // across
-    sources = []
-    for e in range(across):
-        at = lax.rem(y + e, across)
-        head = pl.ds(pl.multiple_of(at * HD, HD), HD)
-        for i, ref in enumerate((key_ref, value_ref)):
-            sources.append((ref.at[:, head], heads[e].at[:, i * HD : (i + 1) * HD]))
-            sources.append((ref.at[:, head], rows[e].at[0:q_rows, i * HD : (i + 1) * HD]))
-        group = pl.ds(pl.multiple_of(at * mine, mine), mine)
-        sources.append((query_ref.at[:, group], rows[e].at[0:q_rows, 2 * HD : 2 * HD + mine]))
-    flags_copy = pltpu.make_async_copy(flags_ref, flags_read, read)
-    flags_copy.start()
-    copies = [
-        pltpu.make_async_copy(source, target, done.at[i])
-        for i, (source, target) in enumerate(sources)
-    ]
-    for copy in copies:
-        copy.start()
-    flags_copy.wait()
-    number = lax.broadcasted_iota(jnp.int32, flags_rows.shape, 0)
-    flags = jnp.zeros(number.shape, jnp.float32)
-    for j in range(flags_read.shape[1]):
-        flags = jnp.where((number == j) & (flags_read[0, j] == 1), 1.0, flags)
-    flags_rows[...] = flags.astype(flags_rows.dtype)
-    for e in range(across):
-        copy = pltpu.make_async_copy(flags_rows, rows[e].at[q_rows:, :], done.at[len(sources) + e])
-        copy.start()
-        copies.append(copy)
-    for copy in copies:
-        copy.wait()
-
-
-def pack(across, keys, values, queries, flags):
-    q_rows, width = queries.shape
-    padded = -(-flags.shape[1] // 16) * 16
-    wide = 2 * HD + width // across
-    head = jax.ShapeDtypeStruct((q_rows, 2 * HD), keys.dtype)
-    row = jax.ShapeDtypeStruct((q_rows + padded, wide), keys.dtype)
-    outs = pl.pallas_call(
-        functools.partial(pack_kernel, across),
-        out_shape=[head] * across + [row] * across,
-        in_specs=[anywhere] * 4,
-        out_specs=[anywhere] * (2 * across),
-        scratch_shapes=[
-            pltpu.SMEM(flags.shape, jnp.int32),
-            pltpu.VMEM((padded, wide), keys.dtype),
-            pltpu.SemaphoreType.DMA((6 * across,)),
-            pltpu.SemaphoreType.DMA(()),
-        ],
-        cost_estimate=small_cost,
-    )(keys, values, queries, flags)
-    return outs[:across], outs[across:]
-
-
-def row_update(turned_ref, blocks_of_row, switches, state, first):
+def pick(rows, number, parts):
+    width = rows.shape[1] // parts
+    picked = rows[:, :width]
+    for part in range(1, parts):
+        picked = jnp.where(number == part, rows[:, part * width : (part + 1) * width], picked)
+    return picked
+
+
+def pair(keys, values):
+    which = lax.broadcasted_iota(jnp.int32, (2,) + keys.shape, 0)
+    return jnp.where(which == 0, keys[None], values[None])
+
+
+def join_kernel(*refs):
+    *parts, out_ref = refs
+    for e, part in enumerate(parts):
+        out_ref[e] = part[...]
+
+
+def join(parts):
+    shape = jax.ShapeDtypeStruct((len(parts),) + parts[0].shape, parts[0].dtype)
+    return call(join_kernel, shape, in_specs=[in_vmem] * len(parts))(*parts)
+
+
+def row_update(turned_ref, kv_ref, switches, state, first):
     top, total_sum, totals = state
     across, _, columns = turned_ref.shape
-    rows = blocks_of_row[0].shape[0]
+    rows = kv_ref.shape[2]
     factor = log_two_e / math.sqrt(HD)
-    keys = jnp.concatenate([kv_ref[0:rows, :HD] for kv_ref in blocks_of_row], axis=0)
-    values = jnp.concatenate([kv_ref[0:rows, HD : 2 * HD] for kv_ref in blocks_of_row], axis=0).T
+    keys = kv_ref[:, 0].reshape(across * rows, HD)
+    values = kv_ref[:, 1].reshape(across * rows, HD).T
     logits = [
         jnp.dot(keys, turned_ref[e], preferred_element_type=jnp.float32) for e in range(across)
     ]
@@ -145,39 +110,28 @@
 
 
 def switch_of(flags_ref, e, owner, columns, allowed=None):
-    padded = flags_ref.shape[0] // 2
-    flag = flags_ref[pl.ds(e * padded + jnp.maximum(owner, 0), 1), :]
+    flag = flags_ref[e, jnp.maximum(owner, 0)] == 1
     if allowed is not None:
-        flag = flag * jnp.where(allowed, 1.0, 0.0)
-    return jnp.concatenate([flag] * (columns // HD), axis=1) > 0.5
-
-
-def first_kernel(across, turns, q_rows, after, meta_ref, *refs):
-    row, refs = refs[:across], refs[across + after :]
-    weight_ref, turned_ref, flags_ref, member_ref, inverse_ref, weight_out = refs[:6]
+        flag = flag & allowed
+    return jnp.full((1, columns), jnp.where(flag, 1, 0), jnp.int32) == 1
+
+
+def first_kernel(across, turns, meta_ref, flags_ref, own_ref, *refs):
+    queries, refs = refs[: across - 1], refs[across - 1 :]
+    kv_ref, weight_ref, turned_ref, member_ref, inverse_ref, weight_out = refs[:6]
     state, rows_ref, copied = refs[6:9], refs[9], refs[10]
-    pieces = copied.shape[0]
-    depth = weight_ref.shape[0] // pieces
-    weight_copies = [
-        pltpu.make_async_copy(
-            weight_ref.at[i * depth : (i + 1) * depth],
-            weight_out.at[i * depth : (i + 1) * depth],
-            copied.at[i],
-        )
-        for i in range(pieces)
-    ]
-    for copy in weight_copies:
-        copy.start()
+    weight_copy = pltpu.make_async_copy(weight_ref, weight_out, copied)
+    weight_copy.start()
     z, y = place(across)
-    repeat = row[0].shape[1] // HD - 2
+    q_rows = kv_ref.shape[2]
+    repeat = own_ref.shape[1] // HD // across
     columns = repeat * q_rows
-    padded = row[0].shape[0] - q_rows
-    for e in range(across):
-        for r in range(repeat):
-            turned_ref[e, :, r * q_rows : (r + 1) * q_rows] = row[e][
-                0:q_rows, (2 + r) * HD : (3 + r) * HD
-            ].T
-        flags_ref[e * padded : (e + 1) * padded, :] = row[e][q_rows:, 0:HD].astype(jnp.float32)
+    for r in range(repeat):
+        span = slice(r * q_rows, (r + 1) * q_rows)
+        head = pl.multiple_of((y * repeat + r) * HD, HD)
+        turned_ref[0, :, span] = own_ref[:, pl.ds(head, HD)].T
+        for e in range(1, across):
+            turned_ref[e, :, span] = queries[e - 1][:, r * HD : (r + 1) * HD].T
     owners = [block_at(z, y, e, across) for e in range(across)]
     switches = [
         [
@@ -186,7 +140,7 @@
         ]
         for e in range(across)
     ]
-    row_update(turned_ref, [ref.at[0:q_rows, 0 : 2 * HD] for ref in row], switches, state, True)
+    row_update(turned_ref, kv_ref, switches, state, True)
 
     column = lax.broadcasted_iota(jnp.int32, (1, columns), 1)
     for e in range(across):
@@ -205,20 +159,18 @@
             member_ref[e, r * turns : (r + 1) * turns, :] = jnp.where(
                 mine, rows_ref[...], 0.0
             ).astype(jnp.bfloat16)
-    for copy in weight_copies:
-        copy.wait()
-
-
-def attend_first(across, turns, q_rows, meta, row, weight, after):
-    padded = row[0].shape[0] - q_rows
-    repeat = row[0].shape[1] // HD - 2
+    weight_copy.wait()
+
+
+def attend_first(across, turns, meta, flags, own, queries, rows, weight):
+    q_rows = rows.shape[2]
+    repeat = own.shape[1] // HD // across
     columns = repeat * q_rows
     f32, b16 = jnp.float32, jnp.bfloat16
     return call(
-        functools.partial(first_kernel, across, turns, q_rows, len(after)),
+        functools.partial(first_kernel, across, turns),
         [
             jax.ShapeDtypeStruct((across, HD, columns), b16),
-            jax.ShapeDtypeStruct((across * padded, HD), f32),
             jax.ShapeDtypeStruct((across, repeat * turns, columns), b16),
             jax.ShapeDtypeStruct((turns, HD), f32),
             jax.ShapeDtypeStruct(weight.shape, weight.dtype),
@@ -226,14 +178,14 @@
             jax.ShapeDtypeStruct((across, 1, columns), f32),
             jax.ShapeDtypeStruct((across, HD, columns), f32),
         ],
-        in_specs=[in_smem] + [in_vmem] * across + [anywhere] * (len(after) + 1),
-        scratch_shapes=[pltpu.VMEM((turns, columns), f32), pltpu.SemaphoreType.DMA((8,))],
+        in_specs=[in_smem] * 2 + [in_vmem] * (across + 1) + [anywhere],
+        scratch_shapes=[pltpu.VMEM((turns, columns), f32), pltpu.SemaphoreType.DMA(())],
         limit=big_limit,
-    )(meta, *row, *after, weight)
-
-
-def next_kernel(across, distance, turns, last, turned_ref, flags_ref, *refs):
-    row, state, refs = refs[:across], refs[across : across + 3], refs[across + 3 :]
+    )(meta, flags, own, *queries, rows, weight)
+
+
+def next_kernel(across, distance, turns, last, flags_ref, turned_ref, kv_ref, *refs):
+    state, refs = refs[:3], refs[3:]
     z, y = place(across)
     columns = turned_ref.shape[2]
 
@@ -244,7 +196,7 @@
             [switch_of(flags_ref, e, owners[b], columns) for b in range(across)]
             for e in range(across)
         ]
-        row_update(turned_ref, row, switches, state, False)
+        row_update(turned_ref, kv_ref, switches, state, False)
 
     if last:
         member_ref, inverse_ref, out_ref = refs
@@ -265,19 +217,19 @@
                 out_ref[s, :, r * HD : (r + 1) * HD] = mean[s * rows : (s + 1) * rows]
 
 
-def attend_next(across, distance, turns, turned, flags, row, state, pool, out_piece):
+def attend_next(across, distance, turns, turned, flags, rows, state, pool, out_piece):
     last = pool is not None
-    args = [turned, flags, *row, *state]
+    args = [flags, turned, rows, *state]
     if last:
         args += list(pool)
         out_shape, aliases = [jax.ShapeDtypeStruct(out_piece, jnp.float32)], {}
     else:
         out_shape = [jax.ShapeDtypeStruct(part.shape, part.dtype) for part in state]
-        aliases = {2 + across + i: i for i in range(len(state))}
+        aliases = {3 + i: i for i in range(len(state))}
     return call(
         functools.partial(next_kernel, across, distance, turns, last),
         out_shape,
-        in_specs=[in_vmem] * len(args),
+        in_specs=[in_smem] + [in_vmem] * (len(args) - 1),
         input_output_aliases=aliases,
     )(*args)
 
@@ -318,23 +270,30 @@
     down = count // across
     turns = turn_lengths.shape[0]
 
-    def send(rows, distance, shift):
-        pairs = []
-        for i in range(count - distance * across):
-            z, y = i // across + distance, (i + shift) % across
-            pairs.append((i, z * across + y))
+    def over(rows, shift):
+        pairs = [(i, i - i % across + (i + shift) % across) for i in range(count)]
         return lax.ppermute(rows, "seq", pairs)
 
+    def up(rows, distance):
+        step = distance * across
+        return lax.ppermute(rows, "seq", [(i, i + step) for i in range(count - step)])
+
+    _, y = place(across)
     my_head = lax.axis_index("head").astype(jnp.int32)
     meta = jnp.concatenate([my_head[None], turn_lengths])
-    parts, row = pack(across, key_states, value_states, queries, block_flags)
-    below = [
-        [send(parts[shift], distance, shift) for shift in range(across)]
-        for distance in range(1, down)
+    heads = []
+    for shift in range(across):
+        at = lax.rem(y + shift, across)
+        heads.append(pair(pick(key_states, at, across), pick(value_states, at, across)))
+    others = [
+        over(pick(queries, lax.rem(y + shift, across), across), shift) for shift in range(1, across)
     ]
-    row = [row[0]] + [send(row[shift], 0, shift) for shift in range(1, across)]
-    turned, flags, member, inverse, weight, *state = attend_first(
-        across, turns, queries.shape[0], meta, row, out_weight, below[-1]
+    rows = join([heads[0]] + [over(heads[shift], shift) for shift in range(1, across)])
+    below = [rows] + [up(rows, distance) for distance in range(1, down)]
+    flags, below[-1] = lax.optimization_barrier((block_flags, below[-1]))
+    flags = jnp.concatenate([flags] + [over(flags, shift) for shift in range(1, across)], axis=0)
+    turned, member, inverse, weight, *state = attend_first(
+        across, turns, meta, flags, queries, others, rows, out_weight
     )
     out_piece = (count, turns // count, queries.shape[1] // across)
     for distance in range(down - 1, 0, -1):
@@ -345,7 +304,7 @@
             turns,
             turned,
             flags,
-            below[distance - 1],
+            below[distance],
             state,
             (member, inverse) if last else None,
             out_piece,

time: 67.4 us -> 49.2 us (0.73)
  Pallas kernels: 32.6 us -> 9.13 us
  waiting for transfers between devices: 0.02 us -> 5.98 us
  starting transfers between devices: 17.7 us -> 14.7 us
  other arithmetic: 1.36 us -> 4.05 us
    pallas_call x2, Pallas kernels: 29.8 us -> 4.73 us  [the longest x1 4.72 us: attend_first(): call(functools.partial(first_kernel, across, turns), [jax.ShapeDtypeStruc...]
    ppermute x7 -> x6, waiting for transfers between devices: 0.02 us -> 5.97 us  [the longest x3 5.96 us: over(): return lax.ppermute(rows, 'seq', pairs)]
    ppermute x7 -> x6, starting transfers between devices: 17.7 us -> 14.7 us  [the longest x3 9.58 us: up(): lax.ppermute(rows, 'seq', [(i, i + step) for i in range(count - step)])]
    select_n x0 -> x3, other arithmetic: none -> 2.02 us  [the longest x2 1.93 us: pick(): jnp.where(number == part, rows[:, part * width:(part + 1) * width], picked)]
    pallas_call x3, Pallas kernels: 0.35 us -> 1.99 us  [attend_next(): call(functools.partial(next_kernel, across, distance, turns, last), out_s...]
  transfers between devices with their start and end apart: 8 -> 7, of which waited for: 0 -> 2; matrix products, arithmetic and copies ran while one was open for 1% -> 5% of each run, Pallas kernels for 9% -> 14%
where the time goes in v3:
time: 49.2 us; the launch traced here: 48.8 us
  starting transfers between devices  14.7 us (30%)
  blocking collectives  13.9 us (28%)
  Pallas kernels  9.13 us (19%)
  waiting for transfers between devices  5.98 us (12%)
  other arithmetic  4.05 us (8%)
  local copies, waits for them, and re-layouts  0.99 us (2%)
    all_to_all x1, blocking collectives, on_device(): lax.all_to_all(state[0], 'seq', split_axis=0, concat_axis=0, tiled=True)  13.9 us
    ppermute x3, starting transfers between devices, up(): lax.ppermute(rows, 'seq', [(i, i + step) for i in range(count - step)])  9.58 us
    ppermute x3, waiting for transfers between devices, over(): return lax.ppermute(rows, 'seq', pairs)  5.96 us
    ppermute x3, starting transfers between devices, over(): return lax.ppermute(rows, 'seq', pairs)  5.12 us
    pallas_call x1, Pallas kernels, attend_first(): call(functools.partial(first_kernel, across, turns), [jax.ShapeDtypeStruc...  4.72 us
    pallas_call x2, Pallas kernels, project(): call(functools.partial(project_kernel, across, other), jax.ShapeDtypeStru...  2.41 us
    pallas_call x3, Pallas kernels, attend_next(): call(functools.partial(next_kernel, across, distance, turns, last), out_s...  1.99 us
    select_n x2, other arithmetic, pick(): jnp.where(number == part, rows[:, part * width:(part + 1) * width], picked)  1.93 us
  transfers between devices with their start and end apart: 7, of which 2 were waited for; matrix products, arithmetic and copies ran while one was open for 5% of the time, Pallas kernels for 14%

profile of v3, /device:TPU:0, one launch (start us, length us, event | category | flops | bytes accessed | tf_op | source)
XLA Modules:
  0.0 48.8 jit_solution(2992564214482713946)
XLA Ops:
  0.0 0.9 %broadcast_select_fusion.2 = (bf16[192,128]{1,0:T(8,128)(2,1)S(1)}, bf16[192,128]{1,0:T(8,128)(2,1)S(1)}, bf16[192,128]{1,0:T(8,128)(2,1)S(1)}, bf16[192,128]{1,0:T(8,128)(2,1)S(1)}) fusion(pred[]{:T(512)S(6)} %eq.18, bf16[192,256]{1,0:T(8,128)(2,1)} %param.8, pred[]{:T(512)S(6)} %eq.17, bf16[192,256]{1,0:T(8,128)(2,1)} %param.7), kind=kLoop, calls=%fused_computation.3 | loop fusion | flops 98304 | bytes 393218 | tf_op jit(solution)/shard_map/jit(_where)/select_n | solution.py:49
  0.9 0.1 broadcast_select_fusion
  1.0 3.0 %collective-permute-start = (bf16[2,192,128]{2,1,0:T(8,128)(2,1)S(1)}, bf16[2,192,128]{2,1,0:T(8,128)(2,1)S(1)}, u32[]{:S(2)}, u32[]{:S(2)}) collective-permute-start(bf16[2,192,128]{2,1,0:T(8,128)(2,1)S(1)} %get-tuple-element.39), channel_id=1, source_target_pairs={{0,2},{2,0},{4,6},{6,4},{8,10},{10,8},{12,14},{14,12},{1,3},{3,1},... | collective-permute-start | bytes 294920 | tf_op jit(solution)/shard_map/ppermute | solution.py:275
  4.0 2.8 %collective-permute-done.refs_1_ = bf16[2,192,128]{2,1,0:T(8,128)(2,1)S(1)} collective-permute-done((bf16[2,192,128]{2,1,0:T(8,128)(2,1)S(1)}, bf16[2,192,128]{2,1,0:T(8,128)(2,1)S(1)}, u32[]{:S(2)}, u32[]{:S(2)}) %collective-permute-start) | collective-permute-done | bytes 98336 | tf_op jit(solution)/shard_map/ppermute | solution.py:275
  6.8 5.8 %collective-permute-start.1 = (bf16[2,2,192,128]{3,2,1,0:T(8,128)(2,1)S(1)}, bf16[2,2,192,128]{3,2,1,0:T(8,128)(2,1)S(1)}, u32[]{:S(2)}, u32[]{:S(2)}) collective-permute-start(bf16[2,2,192,128]{3,2,1,0:T(8,128)(2,1)S(1)} %shard_map.64.refs_1_), channel_id=1, source_target_pairs={{0,12},{2,14},{1,13},{3,15},{16,28},{18,30},{17,29},{19,31}} | collective-permute-start | bytes 589832 | tf_op jit(solution)/shard_map/ppermute | solution.py:279
  12.7 1.0 %slice_select_fusion = bf16[192,512]{1,0:T(8,128)(2,1)S(1)} fusion(bf16[192,1024]{1,0:T(8,128)(2,1)} %own_ref.1, pred[]{:T(512)S(6)} %eq.18), kind=kLoop, calls=%fused_computation | loop fusion | flops 98304 | bytes 589825 | tf_op jit(solution)/shard_map/jit(_where)/select_n | solution.py:49
  13.7 1.6 %collective-permute-start.3 = (bf16[192,512]{1,0:T(8,128)(2,1)S(1)}, bf16[192,512]{1,0:T(8,128)(2,1)S(1)}, u32[]{:S(2)}, u32[]{:S(2)}) collective-permute-start(bf16[192,512]{1,0:T(8,128)(2,1)S(1)} %slice_select_fusion), channel_id=1, source_target_pairs={{0,2},{2,0},{4,6},{6,4},{8,10},{10,8},{12,14},{14,12},{1,3},{3,1},... | collective-permute-start | bytes 589832 | tf_op jit(solution)/shard_map/ppermute | solution.py:275
  15.3 1.3 %collective-permute-start.5 = (bf16[2,2,192,128]{3,2,1,0:T(8,128)(2,1)S(1)}, bf16[2,2,192,128]{3,2,1,0:T(8,128)(2,1)S(1)}, u32[]{:S(2)}, u32[]{:S(2)}) collective-permute-start(bf16[2,2,192,128]{3,2,1,0:T(8,128)(2,1)S(1)} %shard_map.64.refs_1_), channel_id=1, source_target_pairs={{0,8},{2,10},{4,12},{6,14},{1,9},{3,11},{5,13},{7,15},{16,24},{18,... | collective-permute-start | bytes 589832 | tf_op jit(solution)/shard_map/ppermute | solution.py:279
  16.6 2.5 %collective-permute-start.4 = (bf16[2,2,192,128]{3,2,1,0:T(8,128)(2,1)S(1)}, bf16[2,2,192,128]{3,2,1,0:T(8,128)(2,1)S(1)}, u32[]{:S(2)}, u32[]{:S(2)}) collective-permute-start(bf16[2,2,192,128]{3,2,1,0:T(8,128)(2,1)S(1)} %shard_map.64.refs_1_), channel_id=1, source_target_pairs={{0,4},{2,6},{4,8},{6,10},{8,12},{10,14},{1,5},{3,7},{5,9},{7,11},{... | collective-permute-start | bytes 589832 | tf_op jit(solution)/shard_map/ppermute | solution.py:279
  19.1 0.7 %pad_add_fusion.1.meta_ref = s32[17]{0:T(128)S(1)} fusion(s32[16]{0:T(128)} %param.10, s32[1]{0:T(128)} %bitcast), kind=kLoop, calls=%fused_computation.8 | loop fusion | flops 17 | bytes 136 | tf_op jit(solution)/shard_map/concatenate | solution.py:283
  19.8 0.0 collective-permute-done.1.kv_ref
  19.8 0.5 %collective-permute-start.2 = (s32[1,8]{1,0:T(1,128)}, s32[1,8]{1,0:T(1,128)S(1)}, u32[]{:S(2)}, u32[]{:S(2)}) collective-permute-start(s32[1,8]{1,0:T(1,128)} %param.11), channel_id=1, source_target_pairs={{0,2},{2,0},{4,6},{6,4},{8,10},{10,8},{12,14},{14,12},{1,3},{3,1},... | collective-permute-start | bytes 104 | tf_op jit(solution)/shard_map/ppermute | solution.py:275
  20.3 3.2 %collective-permute-done.2 = s32[1,8]{1,0:T(1,128)S(1)} collective-permute-done((s32[1,8]{1,0:T(1,128)}, s32[1,8]{1,0:T(1,128)S(1)}, u32[]{:S(2)}, u32[]{:S(2)}) %collective-permute-start.2) | collective-permute-done | bytes 64 | tf_op jit(solution)/shard_map/ppermute | solution.py:275
  23.5 0.7 %pad_add_fusion.flags_ref = s32[2,8]{1,0:T(2,128)S(1)} fusion(s32[1,8]{1,0:T(1,128)S(1)} %collective-permute-done.2, s32[1,8]{1,0:T(1,128)} %param.11), kind=kLoop, calls=%fused_computation.7 | loop fusion | flops 16 | bytes 128 | tf_op jit(solution)/shard_map/concatenate | solution.py:294
  24.1 0.0 collective-permute-done.3.refs_0_
  24.2 0.0 copy-start
  24.2 1.0 %copy-done = bf16[192,1024]{1,0:T(8,128)(2,1)S(1)} copy-done((bf16[192,1024]{1,0:T(8,128)(2,1)S(1)}, bf16[192,1024]{1,0:T(8,128)(2,1)}, u32[]{:S(2)}) %copy-start) | copy-done | bytes 393240
  25.2 4.7 %shard_map.65 = (bf16[2,128,768]{2,1,0:T(8,128)(2,1)S(1)}, bf16[2,64,768]{2,1,0:T(8,128)(2,1)S(1)}, f32[16,128]{1,0:T(8,128)S(1)}, bf16[1024,4096]{1,0:T(8,128)(...) custom-call(s32[17]{0:T(128)S(1)} %pad_add_fusion.1.meta_ref, ...), custom_call_target="tpu_custom_call" | custom-call | flops 1024 | bytes 1024 | tf_op jit(solution)/shard_map/pallas_call | solution.py:170
  29.9 0.6 %shard_map.66 = (f32[2,1,768]{2,1,0:T(1,128)S(1)}, f32[2,1,768]{2,1,0:T(1,128)S(1)}, f32[2,128,768]{2,1,0:T(8,128)S(1)}) custom-call(s32[2,8]{1,0:T(2,128)S(1)} %pad_add_fusion.flags_ref, bf16[2,128,768]{2,1,0:T(8,128)(2,1)S(1)} %get-tuple-element.21.turned_ref, ...), custom_call_target="tpu_custom_call", output_to_operand_aliasing={{0}: (3, {}), {1}: (4, {}), {2}: (5, {})} | custom-call | flops 1024 | bytes 1024 | tf_op jit(solution)/shard_map/pallas_call | solution.py:229
  30.5 0.0 collective-permute-done.5.kv_ref
  30.5 0.6 %shard_map.67 = (f32[2,1,768]{2,1,0:T(1,128)S(1)}, f32[2,1,768]{2,1,0:T(1,128)S(1)}, f32[2,128,768]{2,1,0:T(8,128)S(1)}) custom-call(s32[2,8]{1,0:T(2,128)S(1)} %pad_add_fusion.flags_ref, bf16[2,128,768]{2,1,0:T(8,128)(2,1)S(1)} %get-tuple-element.21.turned_ref, ...), custom_call_target="tpu_custom_call", output_to_operand_aliasing={{0}: (3, {}), {1}: (4, {}), {2}: (5, {})} | custom-call | flops 1024 | bytes 1024 | tf_op jit(solution)/shard_map/pallas_call | solution.py:229
  31.0 0.0 collective-permute-done.4.kv_ref
  31.1 0.8 %shard_map.68 = f32[8,2,512]{2,1,0:T(2,128)S(1)} custom-call(s32[2,8]{1,0:T(2,128)S(1)} %pad_add_fusion.flags_ref, bf16[2,128,768]{2,1,0:T(8,128)(2,1)S(1)} %get-tuple-element.21.turned_ref, bf16[2,2,192,128]{3,2,1,0:T(8,128)(2,1)S(1)} %collective-permute-done.4.kv_ref, f32[2,1,768]{2,1,0:T(1,128)S(1)} %get-tuple-element.29.refs_0_, ...), custom_call_target="tpu_custom_call" | custom-call | flops 1024 | bytes 1024 | tf_op jit(solution)/shard_map/pallas_call | solution.py:229
  31.9 13.9 %all_to_all.5.parts_ref = f32[8,2,512]{2,1,0:T(2,128)S(1)} all-to-all(f32[8,2,512]{2,1,0:T(2,128)S(1)} %shard_map.68), channel_id=1, replica_groups=mesh['conv'=2,'seq'=8,'head'=2] {'seq'}, dimensions={0} | all-to-all | bytes 65536 | tf_op jit(solution)/shard_map/all_to_all | solution.py:312
  45.8 1.2 %shard_map.70 = f32[2,2048]{1,0:T(2,128)S(1)} custom-call(s32[17]{0:T(128)S(1)} %pad_add_fusion.1.meta_ref, f32[8,2,512]{2,1,0:T(2,128)S(1)} %all_to_all.5.parts_ref, bf16[1024,4096]{1,0:T(8,128)(2,1)S(1)} %get-tuple-element.34.weight_ref), custom_call_target="tpu_custom_call" | custom-call | flops 1024 | bytes 1024 | tf_op jit(solution)/shard_map/pallas_call | solution.py:261
  47.0 0.0 collective-permute-start.6
  47.0 1.2 %shard_map.69 = f32[2,2048]{1,0:T(2,128)S(1)} custom-call(s32[17]{0:T(128)S(1)} %pad_add_fusion.1.meta_ref, f32[8,2,512]{2,1,0:T(2,128)S(1)} %all_to_all.5.parts_ref, bf16[1024,4096]{1,0:T(8,128)(2,1)S(1)} %get-tuple-element.34.weight_ref), custom_call_target="tpu_custom_call" | custom-call | flops 1024 | bytes 1024 | tf_op jit(solution)/shard_map/pallas_call | solution.py:261
  48.2 0.0 collective-permute-done.6
  48.2 0.6 %add.8 = f32[2,2048]{1,0:T(2,128)} add(f32[2,2048]{1,0:T(2,128)S(1)} %shard_map.69, f32[2,2048]{1,0:T(2,128)S(1)} %collective-permute-done.6) | non-fusion elementwise | flops 4096 | bytes 49152 | tf_op jit(solution)/shard_map/add | solution.py:315
  (2 shorter events, 0.0 us)
Async XLA Ops:
  1.0 5.8 %collective-permute-start = (bf16[2,192,128]{2,1,0:T(8,128)(2,1)S(1)}, bf16[2,192,128]{2,1,0:T(8,128)(2,1)S(1)}, u32[]{:S(2)}, u32[]{:S(2)}) collective-permute-start(bf16[2,192,128]{2,1,0:T(8,128)(2,1)S(1)} %get-tuple-element.39), channel_id=1, source_target_pairs={{0,2},{2,0},{4,6},{6,4},{8,10},{10,8},{12,14},{14,12},{1,3},{3,1},... | collective-permute-start | bytes 294920 | tf_op jit(solution)/shard_map/ppermute | solution.py:275
  6.8 13.0 %collective-permute-start.1 = (bf16[2,2,192,128]{3,2,1,0:T(8,128)(2,1)S(1)}, bf16[2,2,192,128]{3,2,1,0:T(8,128)(2,1)S(1)}, u32[]{:S(2)}, u32[]{:S(2)}) collective-permute-start(bf16[2,2,192,128]{3,2,1,0:T(8,128)(2,1)S(1)} %shard_map.64.refs_1_), channel_id=1, source_target_pairs={{0,12},{2,14},{1,13},{3,15},{16,28},{18,30},{17,29},{19,31}} | collective-permute-start | bytes 589832 | tf_op jit(solution)/shard_map/ppermute | solution.py:279
  13.7 10.4 %collective-permute-start.3 = (bf16[192,512]{1,0:T(8,128)(2,1)S(1)}, bf16[192,512]{1,0:T(8,128)(2,1)S(1)}, u32[]{:S(2)}, u32[]{:S(2)}) collective-permute-start(bf16[192,512]{1,0:T(8,128)(2,1)S(1)} %slice_select_fusion), channel_id=1, source_target_pairs={{0,2},{2,0},{4,6},{6,4},{8,10},{10,8},{12,14},{14,12},{1,3},{3,1},... | collective-permute-start | bytes 589832 | tf_op jit(solution)/shard_map/ppermute | solution.py:275
  15.3 15.2 %collective-permute-start.5 = (bf16[2,2,192,128]{3,2,1,0:T(8,128)(2,1)S(1)}, bf16[2,2,192,128]{3,2,1,0:T(8,128)(2,1)S(1)}, u32[]{:S(2)}, u32[]{:S(2)}) collective-permute-start(bf16[2,2,192,128]{3,2,1,0:T(8,128)(2,1)S(1)} %shard_map.64.refs_1_), channel_id=1, source_target_pairs={{0,8},{2,10},{4,12},{6,14},{1,9},{3,11},{5,13},{7,15},{16,24},{18,... | collective-permute-start | bytes 589832 | tf_op jit(solution)/shard_map/ppermute | solution.py:279
  16.6 14.5 %collective-permute-start.4 = (bf16[2,2,192,128]{3,2,1,0:T(8,128)(2,1)S(1)}, bf16[2,2,192,128]{3,2,1,0:T(8,128)(2,1)S(1)}, u32[]{:S(2)}, u32[]{:S(2)}) collective-permute-start(bf16[2,2,192,128]{3,2,1,0:T(8,128)(2,1)S(1)} %shard_map.64.refs_1_), channel_id=1, source_target_pairs={{0,4},{2,6},{4,8},{6,10},{8,12},{10,14},{1,5},{3,7},{5,9},{7,11},{... | collective-permute-start | bytes 589832 | tf_op jit(solution)/shard_map/ppermute | solution.py:279
  19.8 3.7 %collective-permute-start.2 = (s32[1,8]{1,0:T(1,128)}, s32[1,8]{1,0:T(1,128)S(1)}, u32[]{:S(2)}, u32[]{:S(2)}) collective-permute-start(s32[1,8]{1,0:T(1,128)} %param.11), channel_id=1, source_target_pairs={{0,2},{2,0},{4,6},{6,4},{8,10},{10,8},{12,14},{14,12},{1,3},{3,1},... | collective-permute-start | bytes 104 | tf_op jit(solution)/shard_map/ppermute | solution.py:275
  24.2 1.0 %copy-start = (bf16[192,1024]{1,0:T(8,128)(2,1)S(1)}, bf16[192,1024]{1,0:T(8,128)(2,1)}, u32[]{:S(2)}) copy-start(bf16[192,1024]{1,0:T(8,128)(2,1)} %own_ref.1) | copy-start | bytes 1179652
  47.0 1.2 %collective-permute-start.6 = (f32[2,2048]{1,0:T(2,128)S(1)}, f32[2,2048]{1,0:T(2,128)S(1)}, u32[]{:S(2)}, u32[]{:S(2)}) collective-permute-start(f32[2,2048]{1,0:T(2,128)S(1)} %shard_map.70), channel_id=1, source_target_pairs={{0,1},{1,0},{2,3},{3,2},{4,5},{5,4},{6,7},{7,6},{8,9},{9,8},{10,11... | collective-permute-start | bytes 49160 | tf_op jit(solution)/shard_map/ppermute | solution.py:314

commit v4 on v3

--- a/solution.py
+++ b/solution.py
@@ -56,50 +56,58 @@
 
 
 def join_kernel(*refs):
-    *parts, out_ref = refs
+    *parts, _, out_ref = refs
     for e, part in enumerate(parts):
         out_ref[e] = part[...]
 
 
-def join(parts):
+def join(parts, after):
     shape = jax.ShapeDtypeStruct((len(parts),) + parts[0].shape, parts[0].dtype)
-    return call(join_kernel, shape, in_specs=[in_vmem] * len(parts))(*parts)
-
-
-def row_update(turned_ref, kv_ref, switches, state, first):
+    return call(join_kernel, shape, in_specs=[in_vmem] * len(parts) + [anywhere])(*parts, after)
+
+
+def rows_update(turned_ref, rows_refs, switches, state, first):
     top, total_sum, totals = state
     across, _, columns = turned_ref.shape
-    rows = kv_ref.shape[2]
+    rows = rows_refs[0].shape[2]
+    count = across * len(rows_refs)
     factor = log_two_e / math.sqrt(HD)
-    keys = kv_ref[:, 0].reshape(across * rows, HD)
-    values = kv_ref[:, 1].reshape(across * rows, HD).T
+    keys = [kv_ref[:, 0].reshape(across * rows, HD) for kv_ref in rows_refs]
+    values = [kv_ref[:, 1].reshape(across * rows, HD).T for kv_ref in rows_refs]
     logits = [
-        jnp.dot(keys, turned_ref[e], preferred_element_type=jnp.float32) for e in range(across)
+        [jnp.dot(part, turned_ref[e], preferred_element_type=jnp.float32) for part in keys]
+        for e in range(across)
     ]
     if first:
         key_pos = lax.broadcasted_iota(jnp.int32, (rows, 1), 0)
         column = lax.broadcasted_iota(jnp.int32, (1, columns), 1)
         causal = key_pos <= lax.rem(column, rows)
     for e in range(across):
-        blocks = [logits[e][b * rows : (b + 1) * rows] for b in range(across)]
+        blocks = [
+            logits[e][b // across][b % across * rows : (b % across + 1) * rows] for b in range(count)
+        ]
         if first:
             blocks[e] = jnp.where(causal, blocks[e], big_negative)
         new_top = None if first else top[e]
-        for b in range(across):
+        for b in range(count):
             block_top = jnp.ceil(jnp.max(blocks[b], axis=0, keepdims=True) * factor)
             if switches[e][b] is not None:
                 block_top = jnp.where(switches[e][b], block_top, big_negative)
             new_top = block_top if new_top is None else jnp.maximum(new_top, block_top)
         weights, block_sum = [], None
-        for b in range(across):
+        for b in range(count):
             against = new_top
             if switches[e][b] is not None:
                 against = jnp.where(switches[e][b], new_top, -big_negative)
             weights.append(jnp.exp2(blocks[b] * factor - against))
             part = jnp.sum(weights[b], axis=0, keepdims=True)
             block_sum = part if block_sum is None else block_sum + part
-        weights = jnp.concatenate([w.astype(jnp.bfloat16) for w in weights], axis=0)
-        update = jnp.dot(values, weights, preferred_element_type=jnp.float32)
+        update = None
+        for i, part in enumerate(values):
+            mine = weights[i * across : (i + 1) * across]
+            mine = jnp.concatenate([w.astype(jnp.bfloat16) for w in mine], axis=0)
+            part = jnp.dot(part, mine, preferred_element_type=jnp.float32)
+            update = part if update is None else update + part
         if not first:
             rescale = jnp.exp2(top[e] - new_top)
             block_sum = total_sum[e] * rescale + block_sum
@@ -110,16 +118,16 @@
 
 
 def switch_of(flags_ref, e, owner, columns, allowed=None):
-    flag = flags_ref[e, jnp.maximum(owner, 0)] == 1
+    flag = flags_ref[e, pl.ds(jnp.maximum(owner, 0), 1), :]
     if allowed is not None:
-        flag = flag & allowed
-    return jnp.full((1, columns), jnp.where(flag, 1, 0), jnp.int32) == 1
-
-
-def first_kernel(across, turns, meta_ref, flags_ref, own_ref, *refs):
+        flag = flag * jnp.where(allowed, 1.0, 0.0)
+    return jnp.concatenate([flag] * (columns // HD), axis=1) > 0.5
+
+
+def first_kernel(across, turns, meta_ref, own_flags_ref, own_ref, *refs):
     queries, refs = refs[: across - 1], refs[across - 1 :]
-    kv_ref, weight_ref, turned_ref, member_ref, inverse_ref, weight_out = refs[:6]
-    state, rows_ref, copied = refs[6:9], refs[9], refs[10]
+    kv_ref, weight_ref, turned_ref, flags_ref, member_ref, inverse_ref, weight_out = refs[:7]
+    state, rows_ref, copied = refs[7:10], refs[10], refs[11]
     weight_copy = pltpu.make_async_copy(weight_ref, weight_out, copied)
     weight_copy.start()
     z, y = place(across)
@@ -131,7 +139,10 @@
         head = pl.multiple_of((y * repeat + r) * HD, HD)
         turned_ref[0, :, span] = own_ref[:, pl.ds(head, HD)].T
         for e in range(1, across):
-            turned_ref[e, :, span] = queries[e - 1][:, r * HD : (r + 1) * HD].T
+            turned_ref[e, :, span] = queries[e - 1][0:q_rows, r * HD : (r + 1) * HD].T
+    flags_ref[0] = own_flags_ref[...]
+    for e in range(1, across):
+        flags_ref[e] = queries[e - 1][q_rows:, 0:HD].astype(jnp.float32)
     owners = [block_at(z, y, e, across) for e in range(across)]
     switches = [
         [
@@ -140,7 +151,7 @@
         ]
         for e in range(across)
     ]
-    row_update(turned_ref, kv_ref, switches, state, True)
+    rows_update(turned_ref, [kv_ref], switches, state, True)
 
     column = lax.broadcasted_iota(jnp.int32, (1, columns), 1)
     for e in range(across):
@@ -171,6 +182,7 @@
         functools.partial(first_kernel, across, turns),
         [
             jax.ShapeDtypeStruct((across, HD, columns), b16),
+            jax.ShapeDtypeStruct((across,) + flags.shape, f32),
             jax.ShapeDtypeStruct((across, repeat * turns, columns), b16),
             jax.ShapeDtypeStruct((turns, HD), f32),
             jax.ShapeDtypeStruct(weight.shape, weight.dtype),
@@ -178,25 +190,34 @@
             jax.ShapeDtypeStruct((across, 1, columns), f32),
             jax.ShapeDtypeStruct((across, HD, columns), f32),
         ],
-        in_specs=[in_smem] * 2 + [in_vmem] * (across + 1) + [anywhere],
+        in_specs=[in_smem] + [in_vmem] * (across + 2) + [anywhere],
         scratch_shapes=[pltpu.VMEM((turns, columns), f32), pltpu.SemaphoreType.DMA(())],
         limit=big_limit,
     )(meta, flags, own, *queries, rows, weight)
 
 
-def next_kernel(across, distance, turns, last, flags_ref, turned_ref, kv_ref, *refs):
+def next_kernel(across, distances, turns, last, flags_ref, turned_ref, *refs):
+    below, refs = refs[: len(distances)], refs[len(distances) :]
     state, refs = refs[:3], refs[3:]
     z, y = place(across)
     columns = turned_ref.shape[2]
 
-    @pl.when(z >= distance)
-    def _():
-        owners = [block_at(z - distance, y, b, across) for b in range(across)]
+    def update(number):
         switches = [
-            [switch_of(flags_ref, e, owners[b], columns) for b in range(across)]
+            [
+                switch_of(flags_ref, e, block_at(z - distance, y, b, across), columns)
+                for distance in distances[:number]
+                for b in range(across)
+            ]
             for e in range(across)
         ]
-        row_update(turned_ref, kv_ref, switches, state, False)
+        rows_update(turned_ref, below[:number], switches, state, False)
+
+    for number, distance in enumerate(distances):
+        if number + 1 == len(distances):
+            pl.when(z >= distance)(functools.partial(update, number + 1))
+        else:
+            pl.when(z == distance)(functools.partial(update, number + 1))
 
     if last:
         member_ref, inverse_ref, out_ref = refs
@@ -217,19 +238,19 @@
                 out_ref[s, :, r * HD : (r + 1) * HD] = mean[s * rows : (s + 1) * rows]
 
 
-def attend_next(across, distance, turns, turned, flags, rows, state, pool, out_piece):
+def attend_next(across, distances, turns, turned, flags, below, state, pool, out_piece):
     last = pool is not None
-    args = [flags, turned, rows, *state]
+    args = [flags, turned, *below, *state]
     if last:
         args += list(pool)
         out_shape, aliases = [jax.ShapeDtypeStruct(out_piece, jnp.float32)], {}
     else:
         out_shape = [jax.ShapeDtypeStruct(part.shape, part.dtype) for part in state]
-        aliases = {3 + i: i for i in range(len(state))}
+        aliases = {2 + len(below) + i: i for i in range(len(state))}
     return call(
-        functools.partial(next_kernel, across, distance, turns, last),
+        functools.partial(next_kernel, across, distances, turns, last),
         out_shape,
-        in_specs=[in_smem] + [in_vmem] * (len(args) - 1),
+        in_specs=[in_vmem] * len(args),
         input_output_aliases=aliases,
     )(*args)
 
@@ -285,26 +306,31 @@
     for shift in range(across):
         at = lax.rem(y + shift, across)
         heads.append(pair(pick(key_states, at, across), pick(value_states, at, across)))
-    others = [
-        over(pick(queries, lax.rem(y + shift, across), across), shift) for shift in range(1, across)
-    ]
-    rows = join([heads[0]] + [over(heads[shift], shift) for shift in range(1, across)])
+    padded = -(-count // 16) * 16
+    flags = jnp.pad(block_flags[0], (0, padded - count))[:, None]
+    sent = []
+    for shift in range(1, across):
+        group = pick(queries, lax.rem(y + shift, across), across)
+        below = jnp.broadcast_to(flags, (padded, group.shape[1])).astype(group.dtype)
+        sent.append(jnp.concatenate([group, below], axis=0))
+    flags = jnp.broadcast_to(flags, (padded, HD)).astype(jnp.float32)
+    others = [over(group, shift) for shift, group in enumerate(sent, 1)]
+    rows = join([heads[0]] + [over(heads[shift], shift) for shift in range(1, across)], sent[0])
     below = [rows] + [up(rows, distance) for distance in range(1, down)]
-    flags, below[-1] = lax.optimization_barrier((block_flags, below[-1]))
-    flags = jnp.concatenate([flags] + [over(flags, shift) for shift in range(1, across)], axis=0)
-    turned, member, inverse, weight, *state = attend_first(
+    turned, flags, member, inverse, weight, *state = attend_first(
         across, turns, meta, flags, queries, others, rows, out_weight
     )
     out_piece = (count, turns // count, queries.shape[1] // across)
-    for distance in range(down - 1, 0, -1):
-        last = distance == 1
+    stages = [[1]] + [list(range(d, min(d + 2, down))) for d in range(2, down, 2)]
+    for distances in stages:
+        last = distances == stages[-1]
         state = attend_next(
             across,
-            distance,
+            distances,
             turns,
             turned,
             flags,
-            below[distance],
+            [below[distance] for distance in distances],
             state,
             (member, inverse) if last else None,
             out_piece,

time: 49.2 us -> 44.9 us (0.913)
  waiting for transfers between devices: 5.98 us -> 0.83 us
  blocking collectives: 13.9 us -> 18.1 us
  starting transfers between devices: 14.7 us -> 12.7 us
  Pallas kernels: 9.13 us -> 7.45 us
    ppermute x3 -> x2, waiting for transfers between devices: 5.96 us -> 0.82 us  [over(): return lax.ppermute(rows, 'seq', pairs)]
    all_to_all x1, blocking collectives: 13.9 us -> 18.1 us  [on_device(): lax.all_to_all(state[0], 'seq', split_axis=0, concat_axis=0, tiled=True)]
    ppermute x3 -> x2, starting transfers between devices: 5.12 us -> 3.11 us  [over(): return lax.ppermute(rows, 'seq', pairs)]
    pallas_call x4 -> x3, Pallas kernels: 2 us -> 0.34 us  [the longest x2 0.32 us: attend_next(): call(functools.partial(next_kernel, across, distances, turns, last), out_...]
    convert_element_type x0 -> x1, other arithmetic: none -> 0.66 us  [on_device(): jnp.broadcast_to(flags, (padded, group.shape[1])).astype(group.dtype)]
    concatenate x1, other arithmetic: 0.66 us -> 0.1 us  [on_device(): sent.append(jnp.concatenate([group, below], axis=0))]
  transfers between devices with their start and end apart: 7 -> 6, of which waited for: 2 -> 1; matrix products, arithmetic and copies ran while one was open for 5% -> 6% of each run, Pallas kernels for 14% -> 13%
where the time goes in v4:
time: 44.9 us; the launch traced here: 44.5 us
  blocking collectives  18.1 us (40%)
  starting transfers between devices  12.7 us (28%)
  Pallas kernels  7.45 us (17%)
  other arithmetic  4.15 us (9%)
  local copies, waits for them, and re-layouts  1.14 us (3%)
  waiting for transfers between devices  0.83 us (2%)
    all_to_all x1, blocking collectives, on_device(): lax.all_to_all(state[0], 'seq', split_axis=0, concat_axis=0, tiled=True)  18.1 us
    ppermute x3, starting transfers between devices, up(): lax.ppermute(rows, 'seq', [(i, i + step) for i in range(count - step)])  9.59 us
    pallas_call x1, Pallas kernels, attend_first(): call(functools.partial(first_kernel, across, turns), [jax.ShapeDtypeStruc...  4.71 us
    ppermute x2, starting transfers between devices, over(): return lax.ppermute(rows, 'seq', pairs)  3.11 us
    pallas_call x2, Pallas kernels, project(): call(functools.partial(project_kernel, across, other), jax.ShapeDtypeStru...  2.41 us
    select_n x2, other arithmetic, pick(): jnp.where(number == part, rows[:, part * width:(part + 1) * width], picked)  1.93 us
    unnamed x2, local copies, waits for them, and re-layouts  1 us
  transfers between devices with their start and end apart: 6, of which 1 were waited for; matrix products, arithmetic and copies ran while one was open for 6% of the time, Pallas kernels for 13%

profile of v4, /device:TPU:0, one launch (start us, length us, event | category | flops | bytes accessed | tf_op | source)
XLA Modules:
  0.0 44.5 jit_solution(16923145918170295060)
XLA Ops:
  0.0 0.9 %broadcast_select_fusion.2 = (bf16[192,128]{1,0:T(8,128)(2,1)S(1)}, bf16[192,128]{1,0:T(8,128)(2,1)S(1)}, bf16[192,128]{1,0:T(8,128)(2,1)S(1)}, bf16[192,128]{1,0:T(8,128)(2,1)S(1)}) fusion(pred[]{:T(512)S(6)} %eq.16, bf16[192,256]{1,0:T(8,128)(2,1)} %param.8, pred[]{:T(512)S(6)} %eq.18, bf16[192,256]{1,0:T(8,128)(2,1)} %param.7), kind=kLoop, calls=%fused_computation.4 | loop fusion | flops 98304 | bytes 393218 | tf_op jit(solution)/shard_map/jit(_where)/select_n | solution.py:49
  0.9 0.1 broadcast_select_fusion
  1.0 3.0 %collective-permute-start.1 = (bf16[2,192,128]{2,1,0:T(8,128)(2,1)S(1)}, bf16[2,192,128]{2,1,0:T(8,128)(2,1)S(1)}, u32[]{:S(2)}, u32[]{:S(2)}) collective-permute-start(bf16[2,192,128]{2,1,0:T(8,128)(2,1)S(1)} %get-tuple-element.31), channel_id=1, source_target_pairs={{0,2},{2,0},{4,6},{6,4},{8,10},{10,8},{12,14},{14,12},{1,3},{3,1},... | collective-permute-start | bytes 294920 | tf_op jit(solution)/shard_map/ppermute | solution.py:296
  4.0 1.0 %slice_select_fusion = bf16[192,512]{1,0:T(8,128)(2,1)S(1)} fusion(bf16[192,1024]{1,0:T(8,128)(2,1)} %own_ref.1, pred[]{:T(512)S(6)} %eq.16), kind=kLoop, calls=%fused_computation.1 | loop fusion | flops 98304 | bytes 589825 | tf_op jit(solution)/shard_map/jit(_where)/select_n | solution.py:49
  5.1 0.7 %pad_convert_fusion = (bf16[16]{0:T(256)(128)(2,1)S(1)}, f32[16]{0:T(128)S(1)}) fusion(s32[8]{0:T(128)} %bitcast.2), kind=kLoop, calls=%fused_computation.10 | loop fusion | flops 32 | bytes 128 | tf_op jit(solution)/shard_map/convert_element_type | solution.py:314
  5.7 0.1 pad.6.clone
  5.8 0.1 pad_maximum_fusion.refs_2_
  5.9 0.1 collective-permute-start
  6.0 0.8 %collective-permute-done.1.refs_1_ = bf16[2,192,128]{2,1,0:T(8,128)(2,1)S(1)} collective-permute-done((bf16[2,192,128]{2,1,0:T(8,128)(2,1)S(1)}, bf16[2,192,128]{2,1,0:T(8,128)(2,1)S(1)}, u32[]{:S(2)}, u32[]{:S(2)}) %collective-permute-start.1) | collective-permute-done | bytes 98336 | tf_op jit(solution)/shard_map/ppermute | solution.py:296
  6.8 3.8 %collective-permute-start.4 = (bf16[2,2,192,128]{3,2,1,0:T(8,128)(2,1)S(1)}, bf16[2,2,192,128]{3,2,1,0:T(8,128)(2,1)S(1)}, u32[]{:S(2)}, u32[]{:S(2)}) collective-permute-start(bf16[2,2,192,128]{3,2,1,0:T(8,128)(2,1)S(1)} %shard_map.64.refs_1_), channel_id=1, source_target_pairs={{0,4},{2,6},{4,8},{6,10},{8,12},{10,14},{1,5},{3,7},{5,9},{7,11},{... | collective-permute-start | bytes 589832 | tf_op jit(solution)/shard_map/ppermute | solution.py:300
  10.6 4.5 %collective-permute-start.2 = (bf16[2,2,192,128]{3,2,1,0:T(8,128)(2,1)S(1)}, bf16[2,2,192,128]{3,2,1,0:T(8,128)(2,1)S(1)}, u32[]{:S(2)}, u32[]{:S(2)}) collective-permute-start(bf16[2,2,192,128]{3,2,1,0:T(8,128)(2,1)S(1)} %shard_map.64.refs_1_), channel_id=1, source_target_pairs={{0,8},{2,10},{4,12},{6,14},{1,9},{3,11},{5,13},{7,15},{16,24},{18,... | collective-permute-start | bytes 589832 | tf_op jit(solution)/shard_map/ppermute | solution.py:300
  15.1 1.3 %collective-permute-start.3 = (bf16[2,2,192,128]{3,2,1,0:T(8,128)(2,1)S(1)}, bf16[2,2,192,128]{3,2,1,0:T(8,128)(2,1)S(1)}, u32[]{:S(2)}, u32[]{:S(2)}) collective-permute-start(bf16[2,2,192,128]{3,2,1,0:T(8,128)(2,1)S(1)} %shard_map.64.refs_1_), channel_id=1, source_target_pairs={{0,12},{2,14},{1,13},{3,15},{16,28},{18,30},{17,29},{19,31}} | collective-permute-start | bytes 589832 | tf_op jit(solution)/shard_map/ppermute | solution.py:300
  16.5 0.7 %pad_add_fusion.meta_ref = s32[17]{0:T(128)S(1)} fusion(s32[16]{0:T(128)} %param.10, s32[1]{0:T(128)} %bitcast), kind=kLoop, calls=%fused_computation.8 | loop fusion | flops 17 | bytes 136 | tf_op jit(solution)/shard_map/concatenate | solution.py:304
  17.2 0.0 collective-permute-done.refs_0_
  17.2 0.1 broadcast_in_dim.45.own_flags_ref
  17.3 0.0 copy-start
  17.3 1.0 %copy-done = bf16[192,1024]{1,0:T(8,128)(2,1)S(1)} copy-done((bf16[192,1024]{1,0:T(8,128)(2,1)S(1)}, bf16[192,1024]{1,0:T(8,128)(2,1)}, u32[]{:S(2)}) %copy-start) | copy-done | bytes 393240
  18.3 4.7 %shard_map.65 = (bf16[2,128,768]{2,1,0:T(8,128)(2,1)S(1)}, f32[2,16,128]{2,1,0:T(8,128)S(1)}, bf16[2,64,768]{2,1,0:T(8,128)(2,1)S(1)}, f32[16,128]{1,0:T(8,128)S...) custom-call(s32[17]{0:T(128)S(1)} %pad_add_fusion.meta_ref, ...), custom_call_target="tpu_custom_call" | custom-call | flops 1024 | bytes 1024 | tf_op jit(solution)/shard_map/pallas_call | solution.py:181
  23.0 0.0 collective-permute-done.4.refs_0_
  23.0 0.0 collective-permute-done.2.refs_0_
  23.0 0.0 collective-permute-done.3.refs_1_
  23.0 0.3 shard_map.67
  23.3 18.1 %all_to_all.5.parts_ref = f32[8,2,512]{2,1,0:T(2,128)S(1)} all-to-all(f32[8,2,512]{2,1,0:T(2,128)S(1)} %shard_map.67), channel_id=1, replica_groups=mesh['conv'=2,'seq'=8,'head'=2] {'seq'}, dimensions={0} | all-to-all | bytes 65536 | tf_op jit(solution)/shard_map/all_to_all | solution.py:338
  41.5 1.2 %shard_map.69 = f32[2,2048]{1,0:T(2,128)S(1)} custom-call(s32[17]{0:T(128)S(1)} %pad_add_fusion.meta_ref, f32[8,2,512]{2,1,0:T(2,128)S(1)} %all_to_all.5.parts_ref, bf16[1024,4096]{1,0:T(8,128)(2,1)S(1)} %get-tuple-element.26.weight_ref), custom_call_target="tpu_custom_call" | custom-call | flops 1024 | bytes 1024 | tf_op jit(solution)/shard_map/pallas_call | solution.py:282
  42.7 0.0 collective-permute-start.5
  42.7 1.2 %shard_map.68 = f32[2,2048]{1,0:T(2,128)S(1)} custom-call(s32[17]{0:T(128)S(1)} %pad_add_fusion.meta_ref, f32[8,2,512]{2,1,0:T(2,128)S(1)} %all_to_all.5.parts_ref, bf16[1024,4096]{1,0:T(8,128)(2,1)S(1)} %get-tuple-element.26.weight_ref), custom_call_target="tpu_custom_call" | custom-call | flops 1024 | bytes 1024 | tf_op jit(solution)/shard_map/pallas_call | solution.py:282
  43.9 0.0 collective-permute-done.5
  43.9 0.6 %add.10 = f32[2,2048]{1,0:T(2,128)} add(f32[2,2048]{1,0:T(2,128)S(1)} %shard_map.68, f32[2,2048]{1,0:T(2,128)S(1)} %collective-permute-done.5) | non-fusion elementwise | flops 4096 | bytes 49152 | tf_op jit(solution)/shard_map/add | solution.py:341
  (3 shorter events, 0.0 us)
Async XLA Ops:
  1.0 5.8 %collective-permute-start.1 = (bf16[2,192,128]{2,1,0:T(8,128)(2,1)S(1)}, bf16[2,192,128]{2,1,0:T(8,128)(2,1)S(1)}, u32[]{:S(2)}, u32[]{:S(2)}) collective-permute-start(bf16[2,192,128]{2,1,0:T(8,128)(2,1)S(1)} %get-tuple-element.31), channel_id=1, source_target_pairs={{0,2},{2,0},{4,6},{6,4},{8,10},{10,8},{12,14},{14,12},{1,3},{3,1},... | collective-permute-start | bytes 294920 | tf_op jit(solution)/shard_map/ppermute | solution.py:296
  5.9 11.3 %collective-permute-start = (bf16[208,512]{1,0:T(8,128)(2,1)S(1)}, bf16[208,512]{1,0:T(8,128)(2,1)S(1)}, u32[]{:S(2)}, u32[]{:S(2)}) collective-permute-start(bf16[208,512]{1,0:T(8,128)(2,1)S(1)} %pad_maximum_fusion.refs_2_), channel_id=1, source_target_pairs={{0,2},{2,0},{4,6},{6,4},{8,10},{10,8},{12,14},{14,12},{1,3},{3,1},... | collective-permute-start | bytes 638984 | tf_op jit(solution)/shard_map/ppermute | solution.py:296
  6.8 16.1 %collective-permute-start.4 = (bf16[2,2,192,128]{3,2,1,0:T(8,128)(2,1)S(1)}, bf16[2,2,192,128]{3,2,1,0:T(8,128)(2,1)S(1)}, u32[]{:S(2)}, u32[]{:S(2)}) collective-permute-start(bf16[2,2,192,128]{3,2,1,0:T(8,128)(2,1)S(1)} %shard_map.64.refs_1_), channel_id=1, source_target_pairs={{0,4},{2,6},{4,8},{6,10},{8,12},{10,14},{1,5},{3,7},{5,9},{7,11},{... | collective-permute-start | bytes 589832 | tf_op jit(solution)/shard_map/ppermute | solution.py:300
  10.6 12.4 %collective-permute-start.2 = (bf16[2,2,192,128]{3,2,1,0:T(8,128)(2,1)S(1)}, bf16[2,2,192,128]{3,2,1,0:T(8,128)(2,1)S(1)}, u32[]{:S(2)}, u32[]{:S(2)}) collective-permute-start(bf16[2,2,192,128]{3,2,1,0:T(8,128)(2,1)S(1)} %shard_map.64.refs_1_), channel_id=1, source_target_pairs={{0,8},{2,10},{4,12},{6,14},{1,9},{3,11},{5,13},{7,15},{16,24},{18,... | collective-permute-start | bytes 589832 | tf_op jit(solution)/shard_map/ppermute | solution.py:300
  15.1 7.9 %collective-permute-start.3 = (bf16[2,2,192,128]{3,2,1,0:T(8,128)(2,1)S(1)}, bf16[2,2,192,128]{3,2,1,0:T(8,128)(2,1)S(1)}, u32[]{:S(2)}, u32[]{:S(2)}) collective-permute-start(bf16[2,2,192,128]{3,2,1,0:T(8,128)(2,1)S(1)} %shard_map.64.refs_1_), channel_id=1, source_target_pairs={{0,12},{2,14},{1,13},{3,15},{16,28},{18,30},{17,29},{19,31}} | collective-permute-start | bytes 589832 | tf_op jit(solution)/shard_map/ppermute | solution.py:300
  17.3 1.0 %copy-start = (bf16[192,1024]{1,0:T(8,128)(2,1)S(1)}, bf16[192,1024]{1,0:T(8,128)(2,1)}, u32[]{:S(2)}) copy-start(bf16[192,1024]{1,0:T(8,128)(2,1)} %own_ref.1) | copy-start | bytes 1179652
  42.7 1.2 %collective-permute-start.5 = (f32[2,2048]{1,0:T(2,128)S(1)}, f32[2,2048]{1,0:T(2,128)S(1)}, u32[]{:S(2)}, u32[]{:S(2)}) collective-permute-start(f32[2,2048]{1,0:T(2,128)S(1)} %shard_map.69), channel_id=1, source_target_pairs={{0,1},{1,0},{2,3},{3,2},{4,5},{5,4},{6,7},{7,6},{8,9},{9,8},{10,11... | collective-permute-start | bytes 49160 | tf_op jit(solution)/shard_map/ppermute | solution.py:340

commit v5 on v4

--- a/solution.py
+++ b/solution.py
@@ -196,28 +196,39 @@
     )(meta, flags, own, *queries, rows, weight)
 
 
-def next_kernel(across, distances, turns, last, flags_ref, turned_ref, *refs):
-    below, refs = refs[: len(distances)], refs[len(distances) :]
-    state, refs = refs[:3], refs[3:]
+def next_kernel(across, down, distances, turns, last, flags_ref, turned_ref, *refs):
+    state_at = len(distances) + (2 in distances)
+    below, state, refs = refs[:state_at], refs[state_at : state_at + 3], refs[state_at + 3 :]
     z, y = place(across)
     columns = turned_ref.shape[2]
 
-    def update(number):
+    def update(rows, from_distances):
         switches = [
             [
                 switch_of(flags_ref, e, block_at(z - distance, y, b, across), columns)
-                for distance in distances[:number]
+                for distance in from_distances
                 for b in range(across)
             ]
             for e in range(across)
         ]
-        rows_update(turned_ref, below[:number], switches, state, False)
-
-    for number, distance in enumerate(distances):
-        if number + 1 == len(distances):
-            pl.when(z >= distance)(functools.partial(update, number + 1))
-        else:
-            pl.when(z == distance)(functools.partial(update, number + 1))
+        rows_update(turned_ref, rows, switches, state, False)
+
+    for number, distance in enumerate(distances, 1):
+        rows = below[:number]
+        final = number == len(distances)
+        here = (z >= distance) if final else (z == distance)
+        if 2 not in distances:
+            pl.when(here)(functools.partial(update, rows, distances[:number]))
+            continue
+        at = distances.index(2)
+        relayed = rows[:at] + below[-1:] + rows[at + 1 :]
+        most = down - 1 if final else distance
+        if most >= down - 1:
+            pl.when(here & (z == down - 1))(
+                functools.partial(update, relayed, distances[:number])
+            )
+        if distance < down - 1:
+            pl.when(here & (z < down - 1))(functools.partial(update, rows, distances[:number]))
 
     if last:
         member_ref, inverse_ref, out_ref = refs
@@ -238,7 +249,7 @@
                 out_ref[s, :, r * HD : (r + 1) * HD] = mean[s * rows : (s + 1) * rows]
 
 
-def attend_next(across, distances, turns, turned, flags, below, state, pool, out_piece):
+def attend_next(across, down, distances, turns, turned, flags, below, state, pool, out_piece):
     last = pool is not None
     args = [flags, turned, *below, *state]
     if last:
@@ -248,7 +259,7 @@
         out_shape = [jax.ShapeDtypeStruct(part.shape, part.dtype) for part in state]
         aliases = {2 + len(below) + i: i for i in range(len(state))}
     return call(
-        functools.partial(next_kernel, across, distances, turns, last),
+        functools.partial(next_kernel, across, down, distances, turns, last),
         out_shape,
         in_specs=[in_vmem] * len(args),
         input_output_aliases=aliases,
@@ -295,9 +306,14 @@
         pairs = [(i, i - i % across + (i + shift) % across) for i in range(count)]
         return lax.ppermute(rows, "seq", pairs)
 
-    def up(rows, distance):
-        step = distance * across
-        return lax.ppermute(rows, "seq", [(i, i + step) for i in range(count - step)])
+    def up(rows, distance, targets):
+        pairs = [
+            ((z - distance) * across + y, z * across + y)
+            for z in targets
+            if z >= distance
+            for y in range(across)
+        ]
+        return lax.ppermute(rows, "seq", pairs)
 
     _, y = place(across)
     my_head = lax.axis_index("head").astype(jnp.int32)
@@ -316,7 +332,10 @@
     flags = jnp.broadcast_to(flags, (padded, HD)).astype(jnp.float32)
     others = [over(group, shift) for shift, group in enumerate(sent, 1)]
     rows = join([heads[0]] + [over(heads[shift], shift) for shift in range(1, across)], sent[0])
-    below = [rows] + [up(rows, distance) for distance in range(1, down)]
+    below = [rows]
+    for distance in range(1, down):
+        below.append(up(rows, distance, range(down - 1 if distance == 2 else down)))
+    relayed = up(below[1], 1, [down - 1])
     turned, flags, member, inverse, weight, *state = attend_first(
         across, turns, meta, flags, queries, others, rows, out_weight
     )
@@ -326,11 +345,12 @@
         last = distances == stages[-1]
         state = attend_next(
             across,
+            down,
             distances,
             turns,
             turned,
             flags,
-            [below[distance] for distance in distances],
+            [below[distance] for distance in distances] + ([relayed] if 2 in distances else []),
             state,
             (member, inverse) if last else None,
             out_piece,

time: 44.9 us -> 42.8 us (0.953)
  blocking collectives: 18.1 us -> 13.8 us
  starting transfers between devices: 12.7 us -> 14.9 us
    all_to_all x1, blocking collectives: 18.1 us -> 13.8 us  [on_device(): lax.all_to_all(state[0], 'seq', split_axis=0, concat_axis=0, tiled=True)]
    ppermute x2, starting transfers between devices: 3.11 us -> 4.62 us  [over(): return lax.ppermute(rows, 'seq', pairs)]
    ppermute x3 -> x4, starting transfers between devices: 9.59 us -> 10.3 us  [up(): return lax.ppermute(rows, 'seq', pairs)]
  transfers between devices with their start and end apart: 6 -> 7, of which waited for: 1 -> 1; matrix products, arithmetic and copies ran while one was open for 6% -> 6% of each run, Pallas kernels for 13% -> 14%
where the time goes in v5:
time: 42.8 us; the launch traced here: 42.4 us
  starting transfers between devices  14.9 us (35%)
  blocking collectives  13.8 us (32%)
  Pallas kernels  7.45 us (17%)
  other arithmetic  4.15 us (10%)
  local copies, waits for them, and re-layouts  1.14 us (3%)
  waiting for transfers between devices  0.92 us (2%)
    all_to_all x1, blocking collectives, on_device(): lax.all_to_all(state[0], 'seq', split_axis=0, concat_axis=0, tiled=True)  13.8 us
    ppermute x4, starting transfers between devices, up(): return lax.ppermute(rows, 'seq', pairs)  10.3 us
    pallas_call x1, Pallas kernels, attend_first(): call(functools.partial(first_kernel, across, turns), [jax.ShapeDtypeStruc...  4.71 us
    ppermute x2, starting transfers between devices, over(): return lax.ppermute(rows, 'seq', pairs)  4.62 us
    pallas_call x2, Pallas kernels, project(): call(functools.partial(project_kernel, across, other), jax.ShapeDtypeStru...  2.41 us
    select_n x2, other arithmetic, pick(): jnp.where(number == part, rows[:, part * width:(part + 1) * width], picked)  1.93 us
    unnamed x2, local copies, waits for them, and re-layouts  1 us
    ppermute x2, waiting for transfers between devices, over(): return lax.ppermute(rows, 'seq', pairs)  0.9 us
  transfers between devices with their start and end apart: 7, of which 1 were waited for; matrix products, arithmetic and copies ran while one was open for 6% of the time, Pallas kernels for 14%

profile of v5, /device:TPU:0, one launch (start us, length us, event | category | flops | bytes accessed | tf_op | source)
XLA Modules:
  0.0 42.4 jit_solution(8974519287742683430)
XLA Ops:
  0.0 0.9 %broadcast_select_fusion.2 = (bf16[192,128]{1,0:T(8,128)(2,1)S(1)}, bf16[192,128]{1,0:T(8,128)(2,1)S(1)}, bf16[192,128]{1,0:T(8,128)(2,1)S(1)}, bf16[192,128]{1,0:T(8,128)(2,1)S(1)}) fusion(pred[]{:T(512)S(6)} %eq.16, bf16[192,256]{1,0:T(8,128)(2,1)} %param.8, pred[]{:T(512)S(6)} %eq.18, bf16[192,256]{1,0:T(8,128)(2,1)} %param.7), kind=kLoop, calls=%fused_computation.4 | loop fusion | flops 98304 | bytes 393218 | tf_op jit(solution)/shard_map/jit(_where)/select_n | solution.py:49
  0.9 0.1 broadcast_select_fusion
  1.0 3.0 %collective-permute-start.1 = (bf16[2,192,128]{2,1,0:T(8,128)(2,1)S(1)}, bf16[2,192,128]{2,1,0:T(8,128)(2,1)S(1)}, u32[]{:S(2)}, u32[]{:S(2)}) collective-permute-start(bf16[2,192,128]{2,1,0:T(8,128)(2,1)S(1)} %get-tuple-element.31), channel_id=1, source_target_pairs={{0,2},{2,0},{4,6},{6,4},{8,10},{10,8},{12,14},{14,12},{1,3},{3,1},... | collective-permute-start | bytes 294920 | tf_op jit(solution)/shard_map/ppermute | solution.py:307
  4.0 1.0 %slice_select_fusion = bf16[192,512]{1,0:T(8,128)(2,1)S(1)} fusion(bf16[192,1024]{1,0:T(8,128)(2,1)} %own_ref.1, pred[]{:T(512)S(6)} %eq.16), kind=kLoop, calls=%fused_computation.1 | loop fusion | flops 98304 | bytes 589825 | tf_op jit(solution)/shard_map/jit(_where)/select_n | solution.py:49
  5.1 0.7 %pad_convert_fusion = (bf16[16]{0:T(256)(128)(2,1)S(1)}, f32[16]{0:T(128)S(1)}) fusion(s32[8]{0:T(128)} %bitcast.2), kind=kLoop, calls=%fused_computation.10 | loop fusion | flops 32 | bytes 128 | tf_op jit(solution)/shard_map/convert_element_type | solution.py:330
  5.7 0.1 pad.6.clone
  5.8 0.1 pad_maximum_fusion.refs_2_
  5.9 0.9 %collective-permute-done.1.refs_1_ = bf16[2,192,128]{2,1,0:T(8,128)(2,1)S(1)} collective-permute-done((bf16[2,192,128]{2,1,0:T(8,128)(2,1)S(1)}, bf16[2,192,128]{2,1,0:T(8,128)(2,1)S(1)}, u32[]{:S(2)}, u32[]{:S(2)}) %collective-permute-start.1) | collective-permute-done | bytes 98336 | tf_op jit(solution)/shard_map/ppermute | solution.py:307
  6.8 3.8 %collective-permute-start.4 = (bf16[2,2,192,128]{3,2,1,0:T(8,128)(2,1)S(1)}, bf16[2,2,192,128]{3,2,1,0:T(8,128)(2,1)S(1)}, u32[]{:S(2)}, u32[]{:S(2)}) collective-permute-start(bf16[2,2,192,128]{3,2,1,0:T(8,128)(2,1)S(1)} %shard_map.64.refs_1_), channel_id=1, source_target_pairs={{0,4},{2,6},{4,8},{6,10},{8,12},{10,14},{1,5},{3,7},{5,9},{7,11},{... | collective-permute-start | bytes 589832 | tf_op jit(solution)/shard_map/ppermute | solution.py:316
  10.6 1.6 %collective-permute-start = (bf16[208,512]{1,0:T(8,128)(2,1)S(1)}, bf16[208,512]{1,0:T(8,128)(2,1)S(1)}, u32[]{:S(2)}, u32[]{:S(2)}) collective-permute-start(bf16[208,512]{1,0:T(8,128)(2,1)S(1)} %pad_maximum_fusion.refs_2_), channel_id=1, source_target_pairs={{0,2},{2,0},{4,6},{6,4},{8,10},{10,8},{12,14},{14,12},{1,3},{3,1},... | collective-permute-start | bytes 638984 | tf_op jit(solution)/shard_map/ppermute | solution.py:307
  12.2 4.5 %collective-permute-start.2 = (bf16[2,2,192,128]{3,2,1,0:T(8,128)(2,1)S(1)}, bf16[2,2,192,128]{3,2,1,0:T(8,128)(2,1)S(1)}, u32[]{:S(2)}, u32[]{:S(2)}) collective-permute-start(bf16[2,2,192,128]{3,2,1,0:T(8,128)(2,1)S(1)} %shard_map.64.refs_1_), channel_id=1, source_target_pairs={{0,8},{2,10},{1,9},{3,11},{16,24},{18,26},{17,25},{19,27}} | collective-permute-start | bytes 589832 | tf_op jit(solution)/shard_map/ppermute | solution.py:316
  16.7 1.3 %collective-permute-start.3 = (bf16[2,2,192,128]{3,2,1,0:T(8,128)(2,1)S(1)}, bf16[2,2,192,128]{3,2,1,0:T(8,128)(2,1)S(1)}, u32[]{:S(2)}, u32[]{:S(2)}) collective-permute-start(bf16[2,2,192,128]{3,2,1,0:T(8,128)(2,1)S(1)} %shard_map.64.refs_1_), channel_id=1, source_target_pairs={{0,12},{2,14},{1,13},{3,15},{16,28},{18,30},{17,29},{19,31}} | collective-permute-start | bytes 589832 | tf_op jit(solution)/shard_map/ppermute | solution.py:316
  18.0 0.0 collective-permute-done.4.refs_0_
  18.0 0.7 %collective-permute-start.5 = (bf16[2,2,192,128]{3,2,1,0:T(8,128)(2,1)S(1)}, bf16[2,2,192,128]{3,2,1,0:T(8,128)(2,1)S(1)}, u32[]{:S(2)}, u32[]{:S(2)}) collective-permute-start(bf16[2,2,192,128]{3,2,1,0:T(8,128)(2,1)S(1)} %collective-permute-done.4.refs_0_), channel_id=1, source_target_pairs={{8,12},{10,14},{9,13},{11,15},{24,28},{26,30},{25,29},{27,31}} | collective-permute-start | bytes 589832 | tf_op jit(solution)/shard_map/ppermute | solution.py:316
  18.7 0.7 %pad_add_fusion.meta_ref = s32[17]{0:T(128)S(1)} fusion(s32[16]{0:T(128)} %param.10, s32[1]{0:T(128)} %bitcast), kind=kLoop, calls=%fused_computation.8 | loop fusion | flops 17 | bytes 136 | tf_op jit(solution)/shard_map/concatenate | solution.py:320
  19.5 0.0 collective-permute-done.refs_0_
  19.5 0.1 broadcast_in_dim.45.own_flags_ref
  19.5 0.0 copy-start
  19.5 1.0 %copy-done = bf16[192,1024]{1,0:T(8,128)(2,1)S(1)} copy-done((bf16[192,1024]{1,0:T(8,128)(2,1)S(1)}, bf16[192,1024]{1,0:T(8,128)(2,1)}, u32[]{:S(2)}) %copy-start) | copy-done | bytes 393240
  20.5 4.7 %shard_map.65 = (bf16[2,128,768]{2,1,0:T(8,128)(2,1)S(1)}, f32[2,16,128]{2,1,0:T(8,128)S(1)}, bf16[2,64,768]{2,1,0:T(8,128)(2,1)S(1)}, f32[16,128]{1,0:T(8,128)S...) custom-call(s32[17]{0:T(128)S(1)} %pad_add_fusion.meta_ref, ...), custom_call_target="tpu_custom_call" | custom-call | flops 1024 | bytes 1024 | tf_op jit(solution)/shard_map/pallas_call | solution.py:181
  25.3 0.0 collective-permute-done.2.refs_0_
  25.3 0.0 collective-permute-done.3.refs_1_
  25.3 0.0 collective-permute-done.5.refs_2_
  25.3 0.3 shard_map.67
  25.6 13.8 %all_to_all.5.parts_ref = f32[8,2,512]{2,1,0:T(2,128)S(1)} all-to-all(f32[8,2,512]{2,1,0:T(2,128)S(1)} %shard_map.67), channel_id=1, replica_groups=mesh['conv'=2,'seq'=8,'head'=2] {'seq'}, dimensions={0} | all-to-all | bytes 65536 | tf_op jit(solution)/shard_map/all_to_all | solution.py:358
  39.4 1.2 %shard_map.69 = f32[2,2048]{1,0:T(2,128)S(1)} custom-call(s32[17]{0:T(128)S(1)} %pad_add_fusion.meta_ref, f32[8,2,512]{2,1,0:T(2,128)S(1)} %all_to_all.5.parts_ref, bf16[1024,4096]{1,0:T(8,128)(2,1)S(1)} %get-tuple-element.26.weight_ref), custom_call_target="tpu_custom_call" | custom-call | flops 1024 | bytes 1024 | tf_op jit(solution)/shard_map/pallas_call | solution.py:293
  40.6 0.0 collective-permute-start.6
  40.6 1.2 %shard_map.68 = f32[2,2048]{1,0:T(2,128)S(1)} custom-call(s32[17]{0:T(128)S(1)} %pad_add_fusion.meta_ref, f32[8,2,512]{2,1,0:T(2,128)S(1)} %all_to_all.5.parts_ref, bf16[1024,4096]{1,0:T(8,128)(2,1)S(1)} %get-tuple-element.26.weight_ref), custom_call_target="tpu_custom_call" | custom-call | flops 1024 | bytes 1024 | tf_op jit(solution)/shard_map/pallas_call | solution.py:293
  41.8 0.0 collective-permute-done.6
  41.8 0.6 %add.10 = f32[2,2048]{1,0:T(2,128)} add(f32[2,2048]{1,0:T(2,128)S(1)} %shard_map.68, f32[2,2048]{1,0:T(2,128)S(1)} %collective-permute-done.6) | non-fusion elementwise | flops 4096 | bytes 49152 | tf_op jit(solution)/shard_map/add | solution.py:361
  (3 shorter events, 0.0 us)
Async XLA Ops:
  1.0 5.8 %collective-permute-start.1 = (bf16[2,192,128]{2,1,0:T(8,128)(2,1)S(1)}, bf16[2,192,128]{2,1,0:T(8,128)(2,1)S(1)}, u32[]{:S(2)}, u32[]{:S(2)}) collective-permute-start(bf16[2,192,128]{2,1,0:T(8,128)(2,1)S(1)} %get-tuple-element.31), channel_id=1, source_target_pairs={{0,2},{2,0},{4,6},{6,4},{8,10},{10,8},{12,14},{14,12},{1,3},{3,1},... | collective-permute-start | bytes 294920 | tf_op jit(solution)/shard_map/ppermute | solution.py:307
  6.8 11.2 %collective-permute-start.4 = (bf16[2,2,192,128]{3,2,1,0:T(8,128)(2,1)S(1)}, bf16[2,2,192,128]{3,2,1,0:T(8,128)(2,1)S(1)}, u32[]{:S(2)}, u32[]{:S(2)}) collective-permute-start(bf16[2,2,192,128]{3,2,1,0:T(8,128)(2,1)S(1)} %shard_map.64.refs_1_), channel_id=1, source_target_pairs={{0,4},{2,6},{4,8},{6,10},{8,12},{10,14},{1,5},{3,7},{5,9},{7,11},{... | collective-permute-start | bytes 589832 | tf_op jit(solution)/shard_map/ppermute | solution.py:316
  10.6 8.8 %collective-permute-start = (bf16[208,512]{1,0:T(8,128)(2,1)S(1)}, bf16[208,512]{1,0:T(8,128)(2,1)S(1)}, u32[]{:S(2)}, u32[]{:S(2)}) collective-permute-start(bf16[208,512]{1,0:T(8,128)(2,1)S(1)} %pad_maximum_fusion.refs_2_), channel_id=1, source_target_pairs={{0,2},{2,0},{4,6},{6,4},{8,10},{10,8},{12,14},{14,12},{1,3},{3,1},... | collective-permute-start | bytes 638984 | tf_op jit(solution)/shard_map/ppermute | solution.py:307
  12.2 13.1 %collective-permute-start.2 = (bf16[2,2,192,128]{3,2,1,0:T(8,128)(2,1)S(1)}, bf16[2,2,192,128]{3,2,1,0:T(8,128)(2,1)S(1)}, u32[]{:S(2)}, u32[]{:S(2)}) collective-permute-start(bf16[2,2,192,128]{3,2,1,0:T(8,128)(2,1)S(1)} %shard_map.64.refs_1_), channel_id=1, source_target_pairs={{0,8},{2,10},{1,9},{3,11},{16,24},{18,26},{17,25},{19,27}} | collective-permute-start | bytes 589832 | tf_op jit(solution)/shard_map/ppermute | solution.py:316
  16.7 8.6 %collective-permute-start.3 = (bf16[2,2,192,128]{3,2,1,0:T(8,128)(2,1)S(1)}, bf16[2,2,192,128]{3,2,1,0:T(8,128)(2,1)S(1)}, u32[]{:S(2)}, u32[]{:S(2)}) collective-permute-start(bf16[2,2,192,128]{3,2,1,0:T(8,128)(2,1)S(1)} %shard_map.64.refs_1_), channel_id=1, source_target_pairs={{0,12},{2,14},{1,13},{3,15},{16,28},{18,30},{17,29},{19,31}} | collective-permute-start | bytes 589832 | tf_op jit(solution)/shard_map/ppermute | solution.py:316
  18.0 7.3 %collective-permute-start.5 = (bf16[2,2,192,128]{3,2,1,0:T(8,128)(2,1)S(1)}, bf16[2,2,192,128]{3,2,1,0:T(8,128)(2,1)S(1)}, u32[]{:S(2)}, u32[]{:S(2)}) collective-permute-start(bf16[2,2,192,128]{3,2,1,0:T(8,128)(2,1)S(1)} %collective-permute-done.4.refs_0_), channel_id=1, source_target_pairs={{8,12},{10,14},{9,13},{11,15},{24,28},{26,30},{25,29},{27,31}} | collective-permute-start | bytes 589832 | tf_op jit(solution)/shard_map/ppermute | solution.py:316
  19.5 1.0 %copy-start = (bf16[192,1024]{1,0:T(8,128)(2,1)S(1)}, bf16[192,1024]{1,0:T(8,128)(2,1)}, u32[]{:S(2)}) copy-start(bf16[192,1024]{1,0:T(8,128)(2,1)} %own_ref.1) | copy-start | bytes 1179652
  40.6 1.2 %collective-permute-start.6 = (f32[2,2048]{1,0:T(2,128)S(1)}, f32[2,2048]{1,0:T(2,128)S(1)}, u32[]{:S(2)}, u32[]{:S(2)}) collective-permute-start(f32[2,2048]{1,0:T(2,128)S(1)} %shard_map.69), channel_id=1, source_target_pairs={{0,1},{1,0},{2,3},{3,2},{4,5},{5,4},{6,7},{7,6},{8,9},{9,8},{10,11... | collective-permute-start | bytes 49160 | tf_op jit(solution)/shard_map/ppermute | solution.py:360

commit v6 on v5

--- a/solution.py
+++ b/solution.py
@@ -13,7 +13,7 @@
 big_negative = -1e30
 log_two_e = 1.4426950408889634
 
-big_limit = 40 * 1024 * 1024
+big_limit = 48 * 1024 * 1024
 small_cost = pl.CostEstimate(flops=1024, bytes_accessed=1024, transcendentals=0)
 
 in_vmem = pl.BlockSpec(memory_space=pltpu.VMEM)
@@ -124,25 +124,28 @@
     return jnp.concatenate([flag] * (columns // HD), axis=1) > 0.5
 
 
-def first_kernel(across, turns, meta_ref, own_flags_ref, own_ref, *refs):
-    queries, refs = refs[: across - 1], refs[across - 1 :]
+def weight_piece(weight_ref, out_ref, start, sem):
+    return pltpu.make_async_copy(weight_ref.at[start : start + out_ref.shape[0]], out_ref, sem)
+
+
+def first_kernel(across, turns, meta_ref, own_flags_ref, *refs):
+    queries, refs = refs[:across], refs[across:]
     kv_ref, weight_ref, turned_ref, flags_ref, member_ref, inverse_ref, weight_out = refs[:7]
     state, rows_ref, copied = refs[7:10], refs[10], refs[11]
-    weight_copy = pltpu.make_async_copy(weight_ref, weight_out, copied)
+    weight_copy = weight_piece(weight_ref, weight_out, 0, copied)
     weight_copy.start()
     z, y = place(across)
     q_rows = kv_ref.shape[2]
-    repeat = own_ref.shape[1] // HD // across
+    repeat = queries[0].shape[1] // HD
     columns = repeat * q_rows
-    for r in range(repeat):
-        span = slice(r * q_rows, (r + 1) * q_rows)
-        head = pl.multiple_of((y * repeat + r) * HD, HD)
-        turned_ref[0, :, span] = own_ref[:, pl.ds(head, HD)].T
-        for e in range(1, across):
-            turned_ref[e, :, span] = queries[e - 1][0:q_rows, r * HD : (r + 1) * HD].T
+    for e in range(across):
+        for r in range(repeat):
+            turned_ref[e, :, r * q_rows : (r + 1) * q_rows] = queries[e][
+                0:q_rows, r * HD : (r + 1) * HD
+            ].T
     flags_ref[0] = own_flags_ref[...]
     for e in range(1, across):
-        flags_ref[e] = queries[e - 1][q_rows:, 0:HD].astype(jnp.float32)
+        flags_ref[e] = queries[e][q_rows:, 0:HD].astype(jnp.float32)
     owners = [block_at(z, y, e, across) for e in range(across)]
     switches = [
         [
@@ -158,7 +161,7 @@
         position = lax.rem(column, q_rows) + owners[e] * q_rows
         start = jnp.int32(0)
         for t in range(turns):
-            length = meta_ref[1 + t]
+            length = meta_ref[t]
             inside = (position >= start) & (position < start + length)
             rows_ref[t : t + 1, :] = jnp.where(inside, 1.0, 0.0)
             if e == 0:
@@ -173,9 +176,9 @@
     weight_copy.wait()
 
 
-def attend_first(across, turns, meta, flags, own, queries, rows, weight):
+def attend_first(across, turns, meta, flags, queries, rows, weight, piece):
     q_rows = rows.shape[2]
-    repeat = own.shape[1] // HD // across
+    repeat = queries[0].shape[1] // HD
     columns = repeat * q_rows
     f32, b16 = jnp.float32, jnp.bfloat16
     return call(
@@ -185,7 +188,7 @@
             jax.ShapeDtypeStruct((across,) + flags.shape, f32),
             jax.ShapeDtypeStruct((across, repeat * turns, columns), b16),
             jax.ShapeDtypeStruct((turns, HD), f32),
-            jax.ShapeDtypeStruct(weight.shape, weight.dtype),
+            jax.ShapeDtypeStruct((piece, weight.shape[1]), weight.dtype),
             jax.ShapeDtypeStruct((across, 1, columns), f32),
             jax.ShapeDtypeStruct((across, 1, columns), f32),
             jax.ShapeDtypeStruct((across, HD, columns), f32),
@@ -193,12 +196,17 @@
         in_specs=[in_smem] + [in_vmem] * (across + 2) + [anywhere],
         scratch_shapes=[pltpu.VMEM((turns, columns), f32), pltpu.SemaphoreType.DMA(())],
         limit=big_limit,
-    )(meta, flags, own, *queries, rows, weight)
-
-
-def next_kernel(across, down, distances, turns, last, flags_ref, turned_ref, *refs):
-    state_at = len(distances) + (2 in distances)
-    below, state, refs = refs[:state_at], refs[state_at : state_at + 3], refs[state_at + 3 :]
+    )(meta, flags, *queries, rows, weight)
+
+
+def next_kernel(across, down, distances, turns, last, weight_at, flags_ref, turned_ref, *refs):
+    below_count = len(distances) + (1 in distances) + (2 in distances)
+    below, state, refs = refs[:below_count], refs[below_count : below_count + 3], refs[below_count + 3 :]
+    if weight_at is not None:
+        weight_ref, weight_out, copied = refs[0], refs[-2], refs[-1]
+        refs = refs[1:-2]
+        weight_copy = weight_piece(weight_ref, weight_out, weight_at, copied)
+        weight_copy.start()
     z, y = place(across)
     columns = turned_ref.shape[2]
 
@@ -213,23 +221,28 @@
         ]
         rows_update(turned_ref, rows, switches, state, False)
 
+    def when(here, rows, number):
+        pl.when(here)(functools.partial(update, rows, distances[:number]))
+
     for number, distance in enumerate(distances, 1):
         rows = below[:number]
         final = number == len(distances)
         here = (z >= distance) if final else (z == distance)
-        if 2 not in distances:
-            pl.when(here)(functools.partial(update, rows, distances[:number]))
-            continue
-        at = distances.index(2)
-        relayed = rows[:at] + below[-1:] + rows[at + 1 :]
-        most = down - 1 if final else distance
-        if most >= down - 1:
-            pl.when(here & (z == down - 1))(
-                functools.partial(update, relayed, distances[:number])
-            )
-        if distance < down - 1:
-            pl.when(here & (z < down - 1))(functools.partial(update, rows, distances[:number]))
-
+        if distances == [1]:
+            even = lax.rem(z, 2) == 0
+            when(here & even, below[:1], number)
+            when(here & jnp.logical_not(even), below[1:], number)
+        elif 2 in distances:
+            at = distances.index(2)
+            if final or distance == down - 1:
+                when(here & (z == down - 1), rows[:at] + below[-1:] + rows[at + 1 :], number)
+            if distance < down - 1:
+                when(here & (z < down - 1), rows, number)
+        else:
+            when(here, rows, number)
+
+    if weight_at is not None:
+        weight_copy.wait()
     if last:
         member_ref, inverse_ref, out_ref = refs
         rows = out_ref.shape[1]
@@ -249,25 +262,39 @@
                 out_ref[s, :, r * HD : (r + 1) * HD] = mean[s * rows : (s + 1) * rows]
 
 
-def attend_next(across, down, distances, turns, turned, flags, below, state, pool, out_piece):
+def attend_next(across, down, distances, turns, turned, flags, below, state, pool, out_piece, weight, at, piece):
     last = pool is not None
     args = [flags, turned, *below, *state]
+    in_specs = [in_vmem] * len(args)
+    aliases, scratch = {}, []
+    if at is not None:
+        args.append(weight)
+        in_specs.append(anywhere)
+        scratch = [pltpu.SemaphoreType.DMA(())]
     if last:
         args += list(pool)
-        out_shape, aliases = [jax.ShapeDtypeStruct(out_piece, jnp.float32)], {}
+        in_specs += [in_vmem] * len(pool)
+        out_shape = [jax.ShapeDtypeStruct(out_piece, jnp.float32)]
     else:
         out_shape = [jax.ShapeDtypeStruct(part.shape, part.dtype) for part in state]
         aliases = {2 + len(below) + i: i for i in range(len(state))}
+    if at is not None:
+        out_shape.append(jax.ShapeDtypeStruct((piece, weight.shape[1]), weight.dtype))
     return call(
-        functools.partial(next_kernel, across, down, distances, turns, last),
+        functools.partial(next_kernel, across, down, distances, turns, last, at),
         out_shape,
-        in_specs=[in_vmem] * len(args),
+        in_specs=in_specs,
+        scratch_shapes=scratch,
         input_output_aliases=aliases,
+        limit=big_limit if at is not None else 16 * 1024 * 1024,
     )(*args)
 
 
-def project_kernel(across, other, meta_ref, parts_ref, weight_ref, out_ref):
-    side = 1 - meta_ref[0] if other else meta_ref[0]
+def project_kernel(across, other, parts_ref, *refs):
+    weights, out_ref = refs[:-1], refs[-1]
+    side = lax.axis_index("head")
+    if other:
+        side = 1 - side
     groups = []
     for y in range(across):
         total = parts_ref[y]
@@ -283,18 +310,25 @@
     step = math.gcd(half, 512)
     for c in range(half // step):
         start = pl.multiple_of(side * half + c * step, step)
-        product = jnp.dot(
-            both, weight_ref[:, pl.ds(start, step)], preferred_element_type=jnp.float32
-        )
+        product, at = None, 0
+        for weight_ref in weights:
+            depth = weight_ref.shape[0]
+            part = jnp.dot(
+                both[:, at : at + depth],
+                weight_ref[:, pl.ds(start, step)],
+                preferred_element_type=jnp.float32,
+            )
+            product = part if product is None else product + part
+            at += depth
         out_ref[:, c * step : (c + 1) * step] = product[:rows] + product[rows:]
 
 
-def project(across, other, meta, parts, weight):
+def project(across, other, parts, weights):
     return call(
         functools.partial(project_kernel, across, other),
-        jax.ShapeDtypeStruct((parts.shape[1], weight.shape[1] // 2), jnp.float32),
-        in_specs=[in_smem, in_vmem, in_vmem],
-    )(meta, parts, weight)
+        jax.ShapeDtypeStruct((parts.shape[1], weights[0].shape[1] // 2), jnp.float32),
+        in_specs=[in_vmem] * (1 + len(weights)),
+    )(parts, *weights)
 
 
 def on_device(count, queries, key_states, value_states, out_weight, turn_lengths, block_flags):
@@ -316,33 +350,47 @@
         return lax.ppermute(rows, "seq", pairs)
 
     _, y = place(across)
-    my_head = lax.axis_index("head").astype(jnp.int32)
-    meta = jnp.concatenate([my_head[None], turn_lengths])
     heads = []
     for shift in range(across):
         at = lax.rem(y + shift, across)
         heads.append(pair(pick(key_states, at, across), pick(value_states, at, across)))
+    meta = lax.optimization_barrier(jnp.concatenate([turn_lengths, block_flags[0]]))
     padded = -(-count // 16) * 16
-    flags = jnp.pad(block_flags[0], (0, padded - count))[:, None]
+    flags = jnp.pad(meta[turns:], (0, padded - count))[:, None]
+    groups = [pick(queries, lax.rem(y + shift, across), across) for shift in range(across)]
     sent = []
-    for shift in range(1, across):
-        group = pick(queries, lax.rem(y + shift, across), across)
-        below = jnp.broadcast_to(flags, (padded, group.shape[1])).astype(group.dtype)
-        sent.append(jnp.concatenate([group, below], axis=0))
+    for group in groups[1:]:
+        under = jnp.broadcast_to(flags, (padded, group.shape[1])).astype(group.dtype)
+        sent.append(jnp.concatenate([group, under], axis=0))
     flags = jnp.broadcast_to(flags, (padded, HD)).astype(jnp.float32)
     others = [over(group, shift) for shift, group in enumerate(sent, 1)]
     rows = join([heads[0]] + [over(heads[shift], shift) for shift in range(1, across)], sent[0])
-    below = [rows]
-    for distance in range(1, down):
-        below.append(up(rows, distance, range(down - 1 if distance == 2 else down)))
-    relayed = up(below[1], 1, [down - 1])
+    nearest = [up(rows, 1, range(parity, down, 2)) for parity in (0, 1)]
+    farther = [
+        up(rows, distance, range(down - 1 if distance == 2 else down))
+        for distance in range(2, down)
+    ]
+    through = (down - 2) % 2
+    *nearest, = lax.optimization_barrier((*nearest, *others))
+    nearest, others = nearest[:2], nearest[2:]
+    relayed = up(nearest[through], 1, [down - 1])
+    depth = out_weight.shape[0]
+    pieces = [3 * depth // 8, 2 * depth // 8, 3 * depth // 8]
     turned, flags, member, inverse, weight, *state = attend_first(
-        across, turns, meta, flags, queries, others, rows, out_weight
+        across, turns, meta, flags, [groups[0], *others], rows, out_weight, pieces[0]
     )
+    weights = [weight]
     out_piece = (count, turns // count, queries.shape[1] // across)
     stages = [[1]] + [list(range(d, min(d + 2, down))) for d in range(2, down, 2)]
-    for distances in stages:
-        last = distances == stages[-1]
+    for number, distances in enumerate(stages):
+        last = number == len(stages) - 1
+        if number == 0:
+            below = nearest
+        else:
+            below = [farther[distance - 2] for distance in distances]
+            if 2 in distances:
+                below.append(relayed)
+        with_weight = last or number == 0
         state = attend_next(
             across,
             down,
@@ -350,15 +398,21 @@
             turns,
             turned,
             flags,
-            [below[distance] for distance in distances] + ([relayed] if 2 in distances else []),
+            below,
             state,
             (member, inverse) if last else None,
             out_piece,
+            out_weight,
+            sum(pieces[: len(weights)]) if with_weight else None,
+            pieces[len(weights)] if with_weight else None,
         )
+        if with_weight:
+            *state, weight = state
+            weights.append(weight)
     parts = lax.all_to_all(state[0], "seq", split_axis=0, concat_axis=0, tiled=True)
-    others = project(across, True, meta, parts, weight)
-    others = lax.ppermute(others, "head", [(0, 1), (1, 0)])
-    return project(across, False, meta, parts, weight) + others
+    theirs = project(across, True, parts, weights)
+    theirs = lax.ppermute(theirs, "head", [(0, 1), (1, 0)])
+    return project(across, False, parts, weights) + theirs
 
 
 def solution(mesh):

time: 42.8 us -> 49.5 us (1.16)
  blocking collectives: 13.8 us -> 21.7 us
  local copies, waits for them, and re-layouts: 1.14 us -> 0.22 us
  starting transfers between devices: 14.9 us -> 14.1 us
  Pallas kernels: 7.45 us -> 8.25 us
  other arithmetic: 4.15 us -> 3.5 us
    all_to_all x1, blocking collectives: 13.8 us -> 21.7 us  [on_device(): lax.all_to_all(state[0], 'seq', split_axis=0, concat_axis=0, tiled=True)]
    pallas_call x2, Pallas kernels: 0.32 us -> 3.79 us  [attend_next(): call(functools.partial(next_kernel, across, down, distances, turns, last,...]
    pallas_call x1, Pallas kernels: 4.71 us -> 3.11 us  [attend_first(): call(functools.partial(first_kernel, across, turns), [jax.ShapeDtypeStruc...]
    ppermute x2, starting transfers between devices: 4.62 us -> 3.11 us  [over(): return lax.ppermute(rows, 'seq', pairs)]
    pallas_call x2, Pallas kernels: 2.41 us -> 1.34 us  [project(): call(functools.partial(project_kernel, across, other), jax.ShapeDtypeStru...]
    unnamed x2 -> x0, local copies, waits for them, and re-layouts: 1 us -> none
    ppermute x4 -> x5, starting transfers between devices: 10.3 us -> 10.9 us  [up(): return lax.ppermute(rows, 'seq', pairs)]
    convert_element_type x1, other arithmetic: 0.66 us -> 0.01 us  [on_device(): jnp.broadcast_to(flags, (padded, group.shape[1])).astype(group.dtype)]
  transfers between devices with their start and end apart: 7 -> 8, of which waited for: 1 -> 2; matrix products, arithmetic and copies ran while one was open for 6% -> 4% of each run, Pallas kernels for 14% -> 11%
where the time goes in v6:
time: 49.5 us; the launch traced here: 49.1 us
  blocking collectives  21.7 us (44%)
  starting transfers between devices  14.1 us (28%)
  Pallas kernels  8.25 us (17%)
  other arithmetic  3.5 us (7%)
  waiting for transfers between devices  1.18 us (2%)
    all_to_all x1, blocking collectives, on_device(): lax.all_to_all(state[0], 'seq', split_axis=0, concat_axis=0, tiled=True)  21.7 us
    ppermute x5, starting transfers between devices, up(): return lax.ppermute(rows, 'seq', pairs)  10.9 us
    pallas_call x2, Pallas kernels, attend_next(): call(functools.partial(next_kernel, across, down, distances, turns, last,...  3.79 us
    ppermute x2, starting transfers between devices, over(): return lax.ppermute(rows, 'seq', pairs)  3.11 us
    pallas_call x1, Pallas kernels, attend_first(): call(functools.partial(first_kernel, across, turns), [jax.ShapeDtypeStruc...  3.11 us
    select_n x2, other arithmetic, pick(): jnp.where(number == part, rows[:, part * width:(part + 1) * width], picked)  1.94 us
    pallas_call x2, Pallas kernels, project(): call(functools.partial(project_kernel, across, other), jax.ShapeDtypeStru...  1.34 us
  transfers between devices with their start and end apart: 8, of which 2 were waited for; matrix products, arithmetic and copies ran while one was open for 4% of the time, Pallas kernels for 11%

profile of v6, /device:TPU:0, one launch (start us, length us, event | category | flops | bytes accessed | tf_op | source)
XLA Modules:
  0.0 49.1 jit_solution(15070888528353653081)
XLA Ops:
  0.0 0.9 %broadcast_select_fusion.4 = (bf16[192,128]{1,0:T(8,128)(2,1)S(1)}, bf16[192,128]{1,0:T(8,128)(2,1)S(1)}, bf16[192,128]{1,0:T(8,128)(2,1)S(1)}, bf16[192,128]{1,0:T(8,128)(2,1)S(1)}) fusion(pred[]{:T(512)S(6)} %eq.19, bf16[192,256]{1,0:T(8,128)(2,1)} %param.8, pred[]{:T(512)S(6)} %eq.17, bf16[192,256]{1,0:T(8,128)(2,1)} %param.7), kind=kLoop, calls=%fused_computation.5 | loop fusion | flops 98304 | bytes 393218 | tf_op jit(solution)/shard_map/jit(_where)/select_n | solution.py:49
  0.9 0.1 broadcast_select_fusion.2
  1.0 3.0 %collective-permute-start = (bf16[2,192,128]{2,1,0:T(8,128)(2,1)S(1)}, bf16[2,192,128]{2,1,0:T(8,128)(2,1)S(1)}, u32[]{:S(2)}, u32[]{:S(2)}) collective-permute-start(bf16[2,192,128]{2,1,0:T(8,128)(2,1)S(1)} %get-tuple-element.47), channel_id=1, source_target_pairs={{0,2},{2,0},{4,6},{6,4},{8,10},{10,8},{12,14},{14,12},{1,3},{3,1},... | collective-permute-start | bytes 294920 | tf_op jit(solution)/shard_map/ppermute | solution.py:341
  4.0 0.7 %pad_add_fusion.meta_ref = s32[24]{0:T(128)S(1)} fusion(s32[8]{0:T(128)} %bitcast.1, s32[16]{0:T(128)} %param.10), kind=kLoop, calls=%fused_computation.9 | loop fusion | flops 24 | bytes 192 | tf_op jit(solution)/shard_map/concatenate | solution.py:357
  4.8 0.1 slice.27
  4.8 1.1 %broadcast_select_fusion = (bf16[192,512]{1,0:T(8,128)(2,1)S(1)}, bf16[192,512]{1,0:T(8,128)(2,1)S(1)}) fusion(pred[]{:T(512)S(6)} %eq.19, bf16[192,1024]{1,0:T(8,128)(2,1)} %param.6, pred[]{:T(512)S(6)} %eq.17), kind=kLoop, calls=%fused_computation.1 | loop fusion | flops 196608 | bytes 786434 | tf_op jit(solution)/shard_map/jit(_where)/select_n | solution.py:49
  5.9 0.1 pad.6.clone
  6.0 0.1 pad_maximum_fusion.refs_2_
  6.1 0.1 collective-permute-start.3
  6.2 0.6 %collective-permute-done.refs_1_ = bf16[2,192,128]{2,1,0:T(8,128)(2,1)S(1)} collective-permute-done((bf16[2,192,128]{2,1,0:T(8,128)(2,1)S(1)}, bf16[2,192,128]{2,1,0:T(8,128)(2,1)S(1)}, u32[]{:S(2)}, u32[]{:S(2)}) %collective-permute-start) | collective-permute-done | bytes 98336 | tf_op jit(solution)/shard_map/ppermute | solution.py:341
  6.8 3.8 %collective-permute-start.2 = (bf16[2,2,192,128]{3,2,1,0:T(8,128)(2,1)S(1)}, bf16[2,2,192,128]{3,2,1,0:T(8,128)(2,1)S(1)}, u32[]{:S(2)}, u32[]{:S(2)}) collective-permute-start(bf16[2,2,192,128]{3,2,1,0:T(8,128)(2,1)S(1)} %shard_map.64.refs_2_), channel_id=1, source_target_pairs={{0,4},{2,6},{8,12},{10,14},{1,5},{3,7},{9,13},{11,15},{16,20},{18,... | collective-permute-start | bytes 589832 | tf_op jit(solution)/shard_map/ppermute | solution.py:350
  10.6 0.7 %collective-permute-start.1 = (bf16[2,2,192,128]{3,2,1,0:T(8,128)(2,1)S(1)}, bf16[2,2,192,128]{3,2,1,0:T(8,128)(2,1)S(1)}, u32[]{:S(2)}, u32[]{:S(2)}) collective-permute-start(bf16[2,2,192,128]{3,2,1,0:T(8,128)(2,1)S(1)} %shard_map.64.refs_2_), channel_id=1, source_target_pairs={{4,8},{6,10},{5,9},{7,11},{20,24},{22,26},{21,25},{23,27}} | collective-permute-start | bytes 589832 | tf_op jit(solution)/shard_map/ppermute | solution.py:350
  11.3 3.3 %collective-permute-start.5 = (bf16[2,2,192,128]{3,2,1,0:T(8,128)(2,1)S(1)}, bf16[2,2,192,128]{3,2,1,0:T(8,128)(2,1)S(1)}, u32[]{:S(2)}, u32[]{:S(2)}) collective-permute-start(bf16[2,2,192,128]{3,2,1,0:T(8,128)(2,1)S(1)} %shard_map.64.refs_2_), channel_id=1, source_target_pairs={{0,12},{2,14},{1,13},{3,15},{16,28},{18,30},{17,29},{19,31}} | collective-permute-start | bytes 589832 | tf_op jit(solution)/shard_map/ppermute | solution.py:350
  14.6 2.5 %collective-permute-start.4 = (bf16[2,2,192,128]{3,2,1,0:T(8,128)(2,1)S(1)}, bf16[2,2,192,128]{3,2,1,0:T(8,128)(2,1)S(1)}, u32[]{:S(2)}, u32[]{:S(2)}) collective-permute-start(bf16[2,2,192,128]{3,2,1,0:T(8,128)(2,1)S(1)} %shard_map.64.refs_2_), channel_id=1, source_target_pairs={{0,8},{2,10},{1,9},{3,11},{16,24},{18,26},{17,25},{19,27}} | collective-permute-start | bytes 589832 | tf_op jit(solution)/shard_map/ppermute | solution.py:350
  17.1 0.0 collective-permute-done.3.refs_1_
  17.1 0.0 collective-permute-done.2.refs_1_
  17.1 0.0 collective-permute-done.1.refs_0_
  17.2 0.7 %collective-permute-start.6 = (bf16[2,2,192,128]{3,2,1,0:T(8,128)(2,1)S(1)}, bf16[2,2,192,128]{3,2,1,0:T(8,128)(2,1)S(1)}, u32[]{:S(2)}, u32[]{:S(2)}) collective-permute-start(bf16[2,2,192,128]{3,2,1,0:T(8,128)(2,1)S(1)} %collective-permute-done.1.refs_0_), channel_id=1, source_target_pairs={{8,12},{10,14},{9,13},{11,15},{24,28},{26,30},{25,29},{27,31}} | collective-permute-start | bytes 589832 | tf_op jit(solution)/shard_map/ppermute | solution.py:350
  17.8 0.1 broadcast_in_dim.41.own_flags_ref
  17.9 3.1 %shard_map.65 = (bf16[2,128,768]{2,1,0:T(8,128)(2,1)S(1)}, f32[2,16,128]{2,1,0:T(8,128)S(1)}, bf16[2,64,768]{2,1,0:T(8,128)(2,1)S(1)}, f32[16,128]{1,0:T(8,128)S...) custom-call(s32[24]{0:T(128)S(1)} %pad_add_fusion.meta_ref, ...), custom_call_target="tpu_custom_call" | custom-call | flops 1024 | bytes 1024 | tf_op jit(solution)/shard_map/pallas_call | solution.py:184
  21.0 1.6 %shard_map.66 = (f32[2,1,768]{2,1,0:T(1,128)S(1)}, f32[2,1,768]{2,1,0:T(1,128)S(1)}, f32[2,128,768]{2,1,0:T(8,128)S(1)}, bf16[256,4096]{1,0:T(8,128)(2,1)S(1)}) custom-call(f32[2,16,128]{2,1,0:T(8,128)S(1)} %get-tuple-element.23.flags_ref, ...), custom_call_target="tpu_custom_call", output_to_operand_aliasing={{0}: (4, {}), {1}: (5, {}), {2}: (6, {})} | custom-call | flops 1024 | bytes 1024 | tf_op jit(solution)/shard_map/pallas_call | solution.py:283
  22.6 0.0 collective-permute-done.5.refs_1_
  22.7 0.0 collective-permute-done.4.refs_0_
  22.7 0.0 collective-permute-done.6.refs_2_
  22.7 2.2 %shard_map.67 = (f32[8,2,512]{2,1,0:T(2,128)S(1)}, bf16[384,4096]{1,0:T(8,128)(2,1)S(1)}) custom-call(f32[2,16,128]{2,1,0:T(8,128)S(1)} %get-tuple-element.23.flags_ref, bf16[2,128,768]{2,1,0:T(8,128)(2,1)S(1)} %get-tuple-element.24.turned_ref, bf16[2,2,192,128]{3,2,1,0:T(8,128)(2,1)S(1)} %collective-permute-done.4.refs_0_, ...), custom_call_target="tpu_custom_call" | custom-call | flops 1024 | bytes 1024 | tf_op jit(solution)/shard_map/pallas_call | solution.py:283
  24.9 21.7 %all_to_all.5.parts_ref = f32[8,2,512]{2,1,0:T(2,128)S(1)} all-to-all(f32[8,2,512]{2,1,0:T(2,128)S(1)} %get-tuple-element.35), channel_id=1, replica_groups=mesh['conv'=2,'seq'=8,'head'=2] {'seq'}, dimensions={0} | all-to-all | bytes 65536 | tf_op jit(solution)/shard_map/all_to_all | solution.py:412
  46.6 0.7 %shard_map.69 = f32[2,2048]{1,0:T(2,128)S(1)} custom-call(f32[8,2,512]{2,1,0:T(2,128)S(1)} %all_to_all.5.parts_ref, bf16[384,4096]{1,0:T(8,128)(2,1)S(1)} %get-tuple-element.36.refs_0_, bf16[256,4096]{1,0:T(8,128)(2,1)S(1)} %get-tuple-element.37.refs_1_, bf16[384,4096]{1,0:T(8,128)(2,1)S(1)} %get-tuple-element.38.refs_2_), custom_call_target="tpu_custom_call" | custom-call | flops 1024 | bytes 1024 | tf_op jit(solution)/shard_map/pallas_call | solution.py:327
  47.3 0.0 collective-permute-start.7
  47.3 0.7 %shard_map.68 = f32[2,2048]{1,0:T(2,128)S(1)} custom-call(f32[8,2,512]{2,1,0:T(2,128)S(1)} %all_to_all.5.parts_ref, bf16[384,4096]{1,0:T(8,128)(2,1)S(1)} %get-tuple-element.36.refs_0_, bf16[256,4096]{1,0:T(8,128)(2,1)S(1)} %get-tuple-element.37.refs_1_, bf16[384,4096]{1,0:T(8,128)(2,1)S(1)} %get-tuple-element.38.refs_2_), custom_call_target="tpu_custom_call" | custom-call | flops 1024 | bytes 1024 | tf_op jit(solution)/shard_map/pallas_call | solution.py:327
  47.9 0.5 %collective-permute-done.7 = f32[2,2048]{1,0:T(2,128)S(1)} collective-permute-done((f32[2,2048]{1,0:T(2,128)S(1)}, f32[2,2048]{1,0:T(2,128)S(1)}, u32[]{:S(2)}, u32[]{:S(2)}) %collective-permute-start.7) | collective-permute-done | bytes 16416 | tf_op jit(solution)/shard_map/ppermute | solution.py:414
  48.5 0.6 %add.10 = f32[2,2048]{1,0:T(2,128)} add(f32[2,2048]{1,0:T(2,128)S(1)} %shard_map.68, f32[2,2048]{1,0:T(2,128)S(1)} %collective-permute-done.7) | non-fusion elementwise | flops 4096 | bytes 49152 | tf_op jit(solution)/shard_map/add | solution.py:415
  (3 shorter events, 0.0 us)
Async XLA Ops:
  1.0 5.8 %collective-permute-start = (bf16[2,192,128]{2,1,0:T(8,128)(2,1)S(1)}, bf16[2,192,128]{2,1,0:T(8,128)(2,1)S(1)}, u32[]{:S(2)}, u32[]{:S(2)}) collective-permute-start(bf16[2,192,128]{2,1,0:T(8,128)(2,1)S(1)} %get-tuple-element.47), channel_id=1, source_target_pairs={{0,2},{2,0},{4,6},{6,4},{8,10},{10,8},{12,14},{14,12},{1,3},{3,1},... | collective-permute-start | bytes 294920 | tf_op jit(solution)/shard_map/ppermute | solution.py:341
  6.1 11.0 %collective-permute-start.3 = (bf16[208,512]{1,0:T(8,128)(2,1)S(1)}, bf16[208,512]{1,0:T(8,128)(2,1)S(1)}, u32[]{:S(2)}, u32[]{:S(2)}) collective-permute-start(bf16[208,512]{1,0:T(8,128)(2,1)S(1)} %pad_maximum_fusion.refs_2_), channel_id=1, source_target_pairs={{0,2},{2,0},{4,6},{6,4},{8,10},{10,8},{12,14},{14,12},{1,3},{3,1},... | collective-permute-start | bytes 638984 | tf_op jit(solution)/shard_map/ppermute | solution.py:341
  6.8 10.3 %collective-permute-start.2 = (bf16[2,2,192,128]{3,2,1,0:T(8,128)(2,1)S(1)}, bf16[2,2,192,128]{3,2,1,0:T(8,128)(2,1)S(1)}, u32[]{:S(2)}, u32[]{:S(2)}) collective-permute-start(bf16[2,2,192,128]{3,2,1,0:T(8,128)(2,1)S(1)} %shard_map.64.refs_2_), channel_id=1, source_target_pairs={{0,4},{2,6},{8,12},{10,14},{1,5},{3,7},{9,13},{11,15},{16,20},{18,... | collective-permute-start | bytes 589832 | tf_op jit(solution)/shard_map/ppermute | solution.py:350
  10.6 6.5 %collective-permute-start.1 = (bf16[2,2,192,128]{3,2,1,0:T(8,128)(2,1)S(1)}, bf16[2,2,192,128]{3,2,1,0:T(8,128)(2,1)S(1)}, u32[]{:S(2)}, u32[]{:S(2)}) collective-permute-start(bf16[2,2,192,128]{3,2,1,0:T(8,128)(2,1)S(1)} %shard_map.64.refs_2_), channel_id=1, source_target_pairs={{4,8},{6,10},{5,9},{7,11},{20,24},{22,26},{21,25},{23,27}} | collective-permute-start | bytes 589832 | tf_op jit(solution)/shard_map/ppermute | solution.py:350
  11.3 11.3 %collective-permute-start.5 = (bf16[2,2,192,128]{3,2,1,0:T(8,128)(2,1)S(1)}, bf16[2,2,192,128]{3,2,1,0:T(8,128)(2,1)S(1)}, u32[]{:S(2)}, u32[]{:S(2)}) collective-permute-start(bf16[2,2,192,128]{3,2,1,0:T(8,128)(2,1)S(1)} %shard_map.64.refs_2_), channel_id=1, source_target_pairs={{0,12},{2,14},{1,13},{3,15},{16,28},{18,30},{17,29},{19,31}} | collective-permute-start | bytes 589832 | tf_op jit(solution)/shard_map/ppermute | solution.py:350
  14.6 8.0 %collective-permute-start.4 = (bf16[2,2,192,128]{3,2,1,0:T(8,128)(2,1)S(1)}, bf16[2,2,192,128]{3,2,1,0:T(8,128)(2,1)S(1)}, u32[]{:S(2)}, u32[]{:S(2)}) collective-permute-start(bf16[2,2,192,128]{3,2,1,0:T(8,128)(2,1)S(1)} %shard_map.64.refs_2_), channel_id=1, source_target_pairs={{0,8},{2,10},{1,9},{3,11},{16,24},{18,26},{17,25},{19,27}} | collective-permute-start | bytes 589832 | tf_op jit(solution)/shard_map/ppermute | solution.py:350
  17.2 5.5 %collective-permute-start.6 = (bf16[2,2,192,128]{3,2,1,0:T(8,128)(2,1)S(1)}, bf16[2,2,192,128]{3,2,1,0:T(8,128)(2,1)S(1)}, u32[]{:S(2)}, u32[]{:S(2)}) collective-permute-start(bf16[2,2,192,128]{3,2,1,0:T(8,128)(2,1)S(1)} %collective-permute-done.1.refs_0_), channel_id=1, source_target_pairs={{8,12},{10,14},{9,13},{11,15},{24,28},{26,30},{25,29},{27,31}} | collective-permute-start | bytes 589832 | tf_op jit(solution)/shard_map/ppermute | solution.py:350
  47.3 1.2 %collective-permute-start.7 = (f32[2,2048]{1,0:T(2,128)S(1)}, f32[2,2048]{1,0:T(2,128)S(1)}, u32[]{:S(2)}, u32[]{:S(2)}) collective-permute-start(f32[2,2048]{1,0:T(2,128)S(1)} %shard_map.69), channel_id=1, source_target_pairs={{0,1},{1,0},{2,3},{3,2},{4,5},{5,4},{6,7},{7,6},{8,9},{9,8},{10,11... | collective-permute-start | bytes 49160 | tf_op jit(solution)/shard_map/ppermute | solution.py:414
